TPU v7x, 32 devices: a whole 2x2x4 slice. The times are simulated.
32 devices in a mesh: rep: 8 (over z, core), tp: 4 (over y, x).
Axes of the slice: x: 2, y: 2, z: 4, core: 2. Of those that a mesh axis runs over, the one named last changes fastest.
Arguments:
- master: float32 [5120, 10240], P(('rep', 'tp')), may hold values from -0.078125 to 0.078125
- first_moment: float32 [5120, 10240], P(('rep', 'tp')), may hold values from -4 to 4
- second_moment: float32 [5120, 10240], P(('rep', 'tp')), may hold values from 0.1 to 4
- grads: bfloat16 [5120, 10240], P(('rep', 'tp')), may hold values from -6 to 6
- embed: bfloat16 [76800, 5120], P('rep', 'tp'), may hold values from -100 to 100
- ln_gain: float32 [5120], replicated, may hold values from 0.25 to 1.75
- post_gain: float32 [5120], replicated, may hold values from 0.25 to 1.75
- cache_keys: bfloat16 [512, 192, 1024], P('rep', None, 'tp'), may hold values from -600 to 600
- stored_values: bfloat16 [512, 192, 1024], P('rep', None, 'tp'), may hold values from -6 to 6
- lengths: int32 [512], P('rep'), may hold values from 2 to 192, as said below
- token_ids: int32 [512, 4], replicated, may hold values from 0 to 76799
Outputs:
- updated: float32 [5120, 10240], P(('rep', 'tp'))
- first: float32 [5120, 10240], P(('rep', 'tp'))
- second: float32 [5120, 10240], P(('rep', 'tp'))
- normed: bfloat16 [512, 4, 5120], P('rep', None, 'tp')
Inputs may be any that keep to these rules, and one draw needn't show every extreme that they name: `lengths`: some row holds 192.
All inputs are finite; a program needn't handle non-finite values.
Results may differ from a plain program's by a relative error of at most 0.0034.
Values may be sent and summed in bfloat16 or wider, within the bound.
No kernel may reach another device: no remote copies, remote signals or barrier semaphores. Data moves between devices by JAX's collectives and lax.ppermute only.
A program may use at most 320 MiB of HBM per device.

v0:
```python
import functools

import jax
import jax.numpy as jnp
from jax import lax
from jax.experimental import pallas as pl
from jax.experimental.pallas import tpu as pltpu
from jax.sharding import PartitionSpec as P

MODEL_WIDTH = 5120
HEAD_SIZE = 128
STEPS = 4
QG = 4
GROUP_WIDTH = 1280
INNER = (QG + 2) * HEAD_SIZE
OUTER = QG * HEAD_SIZE
SLOTS = 192
ROW_SLOTS = 48


beta_one = 0.9
beta_two = 0.95
learn_rate = 0.001
adam_eps = 1e-08
norm_eps = 1e-06
correct_one = 1.0 - 0.9**10
correct_two = 1.0 - 0.95**10
masked_score = -1e30


def adam_body(master, moment, variance, grads, *refs):
    updated, first, second, serving = refs[-4:]
    slope = grads[...].astype(jnp.float32)
    new_first = beta_one * moment[...] + (1.0 - beta_one) * slope
    new_second = beta_two * variance[...] + (1.0 - beta_two) * slope * slope
    new = master[...] - learn_rate * (new_first / correct_one) / (
        jnp.sqrt(new_second / correct_two) + adam_eps
    )
    first[...] = new_first
    second[...] = new_second
    updated[...] = new
    serving[0] = new.astype(jnp.bfloat16)


def adam(inputs, partial, n_tp, offset, width):
    rows, columns = inputs[0].shape
    groups = columns // GROUP_WIDTH
    local = groups // n_tp
    part = pl.BlockSpec(
        (pl.Element(rows), pl.Element(width)), lambda g: (0, pl.multiple_of(g * GROUP_WIDTH + offset, 256))
    )
    f32 = jax.ShapeDtypeStruct((rows, columns), jnp.float32)
    return pl.pallas_call(
        adam_body,
        grid=(groups,),
        in_specs=[part] * 4 + [pl.BlockSpec(memory_space=pl.ANY)] * len(partial),
        out_specs=[part] * 3
        + [pl.BlockSpec((1, rows, width), lambda g: (g // local, 0, g % local))],
        out_shape=[f32] * 3 + [jax.ShapeDtypeStruct((n_tp, rows, local * width), jnp.bfloat16)],
        input_output_aliases={4 + i: i for i in range(len(partial))},
        compiler_params=pltpu.CompilerParams(vmem_limit_bytes=56 * 2**20),
        cost_estimate=pl.CostEstimate(
            flops=15 * rows * groups * width,
            bytes_accessed=28 * rows * groups * width,
            transcendentals=0,
        ),
    )(*inputs, *partial)


BATCH = 96


def gather_body(ids, embed, out, blocks, stage, found, sems):
    batches = blocks.shape[0]

    def start(batch):
        def one(slot, carry):
            tile = pl.multiple_of((ids[batch * BATCH + slot] >> 4) * 16, 16)
            pltpu.make_async_copy(
                embed.at[pl.ds(tile, 16)],
                blocks.at[batch, pl.ds(pl.multiple_of(slot * 16, 16), 16)],
                sems.at[batch],
            ).start()
            return carry

        lax.fori_loop(0, BATCH, one, 0, unroll=8)

    def pick(batch):
        pltpu.make_async_copy(
            embed.at[pl.ds(0, BATCH * 16)], blocks.at[batch], sems.at[batch]
        ).wait()

        def some(turn, carry):
            for lane in range(8):
                slot = turn * 8 + lane
                tile = blocks[batch, pl.ds(pl.multiple_of(slot * 16, 16), 16)]
                stage[lane] = tile.astype(jnp.float32)
            for lane in range(8):
                slot = batch * BATCH + turn * 8 + lane
                found[pl.ds(slot, 1)] = stage[lane, pl.ds(ids[slot] & 15, 1)]
            return carry

        lax.fori_loop(0, BATCH // 8, some, 0)

    for batch in range(batches):
        start(batch)
    for batch in range(batches):
        pick(batch)
    out[...] = found[...].astype(out.dtype)


def gather_rows(embed, ids):
    slots, width = ids.shape[0], embed.shape[1]
    batches = slots // BATCH
    return pl.pallas_call(
        gather_body,
        grid_spec=pltpu.PrefetchScalarGridSpec(
            num_scalar_prefetch=1,
            grid=(1,),
            in_specs=[pl.BlockSpec(memory_space=pl.ANY)],
            out_specs=pl.BlockSpec((slots, width), lambda i, _: (0, 0)),
            scratch_shapes=[
                pltpu.VMEM((batches, BATCH * 16, width), embed.dtype),
                pltpu.VMEM((8, 16, width), jnp.float32),
                pltpu.VMEM((slots, width), jnp.float32),
                pltpu.SemaphoreType.DMA((batches,)),
            ],
        ),
        out_shape=jax.ShapeDtypeStruct((slots, width), embed.dtype),
        compiler_params=pltpu.CompilerParams(vmem_limit_bytes=56 * 2**20),
        cost_estimate=pl.CostEstimate(
            flops=0, bytes_accessed=40 * slots * width, transcendentals=0
        ),
    )(ids, embed)


def attend_body(lengths, queries, fresh_keys, fresh_values, keys, values, heads, *, block_row):
    rows, groups, lines, width = queries.shape
    places = keys.shape[1]
    scale = width ** (-0.5)
    start = block_row(pl.program_id(0)) * rows
    column = lax.broadcasted_iota(jnp.int32, (lines, places), 1)
    step_of = lax.broadcasted_iota(jnp.int32, (lines, lines), 0) // QG
    causal = lax.broadcasted_iota(jnp.int32, (lines, lines), 1) <= step_of
    across = (((1,), (1,)), ((), ()))
    scores = []
    for row in range(rows):
        live = column < lengths[start + row]
        for group in range(groups):
            at = slice(group * width, (group + 1) * width)
            query = queries[row, group]
            cached = lax.dot_general(
                query, keys[row, :, at], across, preferred_element_type=jnp.float32
            )
            fresh = lax.dot_general(
                query, fresh_keys[row, group], across, preferred_element_type=jnp.float32
            )
            cached = jnp.where(live, cached * scale, masked_score)
            fresh = jnp.where(causal, fresh * scale, masked_score)
            scores.append((cached, fresh))
    probs = []
    for cached, fresh in scores:
        top = jnp.maximum(
            jnp.max(cached, axis=-1, keepdims=True), jnp.max(fresh, axis=-1, keepdims=True)
        )
        cached = jnp.exp(cached - top)
        fresh = jnp.exp(fresh - top)
        total = jnp.sum(cached, axis=-1, keepdims=True) + jnp.sum(fresh, axis=-1, keepdims=True)
        probs.append(((cached / total).astype(jnp.bfloat16), (fresh / total).astype(jnp.bfloat16)))
    for row in range(rows):
        for group in range(groups):
            at = slice(group * width, (group + 1) * width)
            cached, fresh = probs[row * groups + group]
            out = jnp.dot(cached, values[row, :, at], preferred_element_type=jnp.float32)
            out = out + jnp.dot(
                fresh, fresh_values[row, group], preferred_element_type=jnp.float32
            )
            heads[row, group] = out.astype(jnp.bfloat16)


def attend(projected, keys, values, lengths, rows, chunk, chunks):
    count, columns = projected.shape
    groups = columns // INNER
    here = count // STEPS
    lines = STEPS * QG
    split = projected.reshape(here, STEPS, groups, INNER).transpose(0, 2, 1, 3)
    queries = split[..., :OUTER].reshape(here, groups, lines, HEAD_SIZE)
    pad = ((0, 0), (0, 0), (0, lines - STEPS), (0, 0))
    fresh_keys = jnp.pad(split[..., OUTER : OUTER + HEAD_SIZE], pad)
    fresh_values = jnp.pad(split[..., OUTER + HEAD_SIZE :], pad)
    places, width = keys.shape[1:]
    block_row = lambda i: i * chunks + chunk
    small = pl.BlockSpec((rows, groups, lines, HEAD_SIZE), lambda i, _: (i, 0, 0, 0))
    cache = pl.BlockSpec((rows, places, width), lambda i, _: (block_row(i), 0, 0))
    heads = pl.pallas_call(
        functools.partial(attend_body, block_row=block_row),
        grid_spec=pltpu.PrefetchScalarGridSpec(
            num_scalar_prefetch=1,
            grid=(here // rows,),
            in_specs=[small, small, small, cache, cache],
            out_specs=small,
        ),
        out_shape=jax.ShapeDtypeStruct(queries.shape, jnp.bfloat16),
        compiler_params=pltpu.CompilerParams(vmem_limit_bytes=56 * 2**20),
        cost_estimate=pl.CostEstimate(
            flops=4 * here * groups * lines * places * HEAD_SIZE,
            bytes_accessed=4 * here * places * width,
            transcendentals=here * groups * lines * places,
        ),
    )(lengths, queries, fresh_keys, fresh_values, keys, values)
    heads = heads.reshape(here, groups, STEPS, OUTER).transpose(0, 2, 1, 3)
    return heads.reshape(count, groups * OUTER)


def flip(values, axis, bit):
    n = lax.axis_size(axis)
    return lax.ppermute(values, axis, [(i, i ^ bit) for i in range(n)])


def hop(values, first, last, step):
    pairs = [(2 * p + core, 2 * (p + step) + core) for p in range(first, last) for core in (0, 1)]
    return lax.ppermute(values, "rep", pairs)


def block_of(values, index):
    return lax.dynamic_index_in_dim(values, index, 0, keepdims=False)


def line_sum(block, plane, planes):
    right = left = None
    for step in range(1, planes):
        forth = block(jnp.minimum(plane + planes - step, planes - 1))
        back = block(jnp.maximum(plane - planes + step, 0))
        if right is not None:
            forth, back = forth + right, back + left
        right = hop(forth.astype(jnp.bfloat16), 0, step, 1)
        left = hop(back.astype(jnp.bfloat16), planes - step, planes, -1)
    return block(plane) + right.astype(jnp.float32) + left.astype(jnp.float32)


def numbers(ids, block):
    count = ids.shape[-1]
    index = jnp.arange(count, dtype=jnp.int32)
    same = ids[..., :, None] == ids[..., None, :]
    leader = jnp.min(jnp.where(same, index[:, None], count), axis=-2)
    first = leader == index
    ahead = (block[..., :, None] == block[..., None, :]) & first[..., :, None]
    ahead = ahead & (index[:, None] < leader[..., None, :])
    return first, jnp.sum(ahead.astype(jnp.int32), axis=-2)


def listed(ids, chosen, number, low, slots):
    at = jnp.where(chosen, number - low, -1)
    hit = at[..., :, None] == jnp.arange(slots, dtype=jnp.int32)
    return jnp.sum(jnp.where(hit, ids[..., :, None], 0), axis=-2)


def placed(rows, block, number, low, slots):
    slot = number - low
    at = jnp.where((slot >= 0) & (slot < slots), block * slots + slot, -1)
    pick = at[:, None] == jnp.arange(rows.shape[0], dtype=jnp.int32)[None, :]
    return jnp.dot(pick.astype(jnp.bfloat16), rows, preferred_element_type=jnp.float32).astype(
        jnp.bfloat16
    )


def in_rounds(rounds, one_round):
    return lax.fori_loop(1, rounds, lambda turn, kept: kept + one_round(turn), one_round(0))


def shards(
    master,
    first_moment,
    second_moment,
    grads,
    embed,
    ln_gain,
    post_gain,
    cache_keys,
    stored_values,
    lengths,
    token_ids,
):
    n_rep = lax.axis_size("rep")
    n_tp = lax.axis_size("tp")
    rep, tp = lax.axis_index("rep"), lax.axis_index("tp")
    planes = n_rep // 2
    plane, core = rep // 2, rep % 2
    vocab_local, width_local = embed.shape
    rows_here = lengths.shape[0]
    count = rows_here * STEPS
    depth = MODEL_WIDTH // n_rep
    swap = lambda values, axis="tp": lax.all_to_all(
        values, axis, split_axis=0, concat_axis=0, tiled=True
    )

    weights_in = (master, first_moment, second_moment, grads)
    *partial, outer = adam(weights_in, (), n_tp, INNER, OUTER)
    outer = swap(outer).reshape(depth, -1)
    out_weights = lax.all_gather(outer, "rep", axis=0, tiled=True)

    token_ids, _ = lax.optimization_barrier((token_ids, partial[0]))
    ids = token_ids.reshape(n_rep, count)
    block = ids // vocab_local
    flat_ids, flat_block = ids.reshape(-1), block.reshape(-1)
    first, number = numbers(flat_ids, flat_block)
    core_tokens = lambda values: lax.dynamic_index_in_dim(
        values.reshape(planes, 2, count), core, 1, keepdims=False
    ).reshape(-1)
    core_block, core_number = core_tokens(flat_block), core_tokens(number)
    local_ids = flat_ids - rep * vocab_local

    def fetch(turn):
        return gather_rows(
            embed, listed(local_ids, first & (flat_block == rep), number, turn * SLOTS, SLOTS)
        )

    rows = fetch(0)
    held = lax.optimization_barrier((*weights_in, *partial, rows))
    updated, new_first, second, inner = adam(held[:4], held[4:7], n_tp, 0, INNER)
    inner = swap(inner).reshape(depth, -1)
    inner_other = flip(inner, "rep", 1)

    def normed_rows(turn):
        found = rows if isinstance(turn, int) else fetch(turn)
        tokens = swap(found.reshape(n_tp, -1, width_local)).astype(jnp.float32)
        mean_sq = jnp.sum(tokens * tokens, axis=(0, 2), keepdims=True) / MODEL_WIDTH
        normed_in = tokens * lax.rsqrt(mean_sq + norm_eps) * ln_gain.reshape(n_tp, 1, width_local)
        normed_in = normed_in.astype(jnp.bfloat16)
        share = normed_in.shape[1]
        normed_in = normed_in.reshape(n_tp, share, n_rep // n_tp, depth).transpose(0, 2, 1, 3)
        got = swap(normed_in.reshape(n_rep, share, depth), "rep")
        got = swap(jnp.broadcast_to(got[None], (n_tp,) + got.shape))
        got = got.transpose(1, 0, 2, 3).reshape(-1, depth)
        other = flip(got, "rep", 1)
        put = lambda values: placed(values, core_block, core_number, turn * SLOTS, SLOTS)
        return jnp.stack([put(got), put(other)])

    rounds = jnp.max(number) // SLOTS + 1
    spread = in_rounds(rounds, normed_rows)
    project = lambda x, w: jnp.dot(x, w, preferred_element_type=jnp.float32)
    terms = project(spread[0], inner) + project(spread[1], inner_other)
    terms = terms.reshape(planes, count, -1)
    projected = line_sum(lambda d: block_of(terms, d), plane, planes).astype(jnp.bfloat16)

    heads = attend(projected, cache_keys, stored_values, lengths, 8, 0, 1)

    row_first, row_number = numbers(ids, block)
    my_block, my_number = block_of(block, rep), block_of(row_number, rep)

    def own_rows(turn):
        low = turn * ROW_SLOTS
        wanted = listed(
            ids - rep * vocab_local, row_first & (block == rep), row_number, low, ROW_SLOTS
        )
        sent = gather_rows(embed, wanted.reshape(-1)).reshape(n_rep, ROW_SLOTS, width_local)
        got = swap(sent, "rep").reshape(-1, width_local)
        return placed(got, my_block, my_number, low, ROW_SLOTS)

    own_cols = in_rounds(jnp.max(row_number) // ROW_SLOTS + 1, own_rows)

    partial_out = jnp.stack(
        [
            lax.dot_general(
                heads,
                out_weights[at * width_local : (at + 1) * width_local],
                (((1,), (1,)), ((), ())),
                preferred_element_type=jnp.float32,
            ).astype(jnp.bfloat16)
            for at in range(n_tp)
        ]
    )
    attended = jnp.sum(swap(partial_out).astype(jnp.float32), axis=0)
    resid = own_cols.astype(jnp.float32) + attended
    square = jnp.sum(resid * resid, axis=-1)
    total = functools.reduce(
        jnp.add, [square] + [flip(square, "tp", other) for other in range(1, n_tp)]
    )
    gain = lax.dynamic_slice_in_dim(post_gain, tp * width_local, width_local, 0)
    normed = resid * lax.rsqrt(total / MODEL_WIDTH + norm_eps)[:, None] * gain
    normed = normed.astype(jnp.bfloat16).reshape(rows_here, STEPS, width_local)
    return (updated, new_first, second, normed)


def solution(mesh):
    return jax.shard_map(
        shards,
        mesh=mesh,
        in_specs=(
            P(("rep", "tp"), None),
            P(("rep", "tp"), None),
            P(("rep", "tp"), None),
            P(("rep", "tp"), None),
            P("rep", "tp"),
            P(),
            P(),
            P("rep", None, "tp"),
            P("rep", None, "tp"),
            P("rep"),
            P(),
        ),
        out_specs=(
            P(("rep", "tp"), None),
            P(("rep", "tp"), None),
            P(("rep", "tp"), None),
            P("rep", None, "tp"),
        ),
        check_vma=False,
    )
```

profile of v0, /device:TPU:0, one launch (start us, length us, event | category | flops | bytes accessed | tf_op | source)
XLA Modules:
  0.0 370.3 jit_solution(3997708013382962736)
XLA Ops:
  7.2 9.2 %shard_map.138 = (f32[160,10240]{1,0:T(8,128)}, f32[160,10240]{1,0:T(8,128)}, f32[160,10240]{1,0:T(8,128)}, bf16[4,160,1024]{2,1,0:T(8,128)(2,1)}) custom-call(f32[160,10240]{1,0:T(8,128)} %master.2, f32[160,10240]{1,0:T(8,128)} %moment.2, f32[160,10240]{1,0:T(8,128)} %variance.2, bf16[160,10240]{1,0:T(8,128)(2,1)} %grads.2), custom_call_target="tpu_custom_call" | custom-call | flops 9830400 | bytes 18350080 | tf_op jit(solution)/shard_map/pallas_call | solution.py:53
  16.8 2.3 select_reduce_fusion.2
  19.1 4.7 %convert_reduce_fusion = s32[2048]{0:T(1024)S(1)} fusion(s32[2048]{0:T(1024)S(1)} %select_reduce_fusion.2, s32[2048]{0:T(1024)S(1)} %add_select_fusion.2, pred[2048]{0:T(1024)(128)(4,1)S(1)} %iota_compare_fusion.33), kind=kLoop, calls=%fused_computation.30 | loop fusion | flops 25163776 | bytes 26624 | tf_op jit(solution)/shard_map/reduce_sum | solution.py:249
  25.4 6.7 %shard_map.139 = bf16[192,1280]{1,0:T(8,128)(2,1)} custom-call(s32[192]{0:T(256)} %select_reduce_fusion.4.ids, bf16[9600,1280]{1,0:T(8,128)(2,1)} %embed.3), custom_call_target="tpu_custom_call" | custom-call | bytes 9830400 | tf_op jit(solution)/shard_map/pallas_call | solution.py:115
  32.1 5.2 %all-to-all-start.5 = ((bf16[4,48,1280]{2,1,0:T(8,128)(2,1)}), bf16[4,48,1280]{2,1,0:T(8,128)(2,1)S(1)}, u32[]{:S(2)}, u32[]{:S(2)}) async-start(bf16[4,48,1280]{2,1,0:T(8,128)(2,1)} %bitcast.132), calls=%async_computation.5 | async-start | bytes 983040 | tf_op jit(solution)/shard_map/all_to_all | solution.py:293
  37.2 7.4 %all-to-all-done.5 = bf16[4,48,1280]{2,1,0:T(8,128)(2,1)S(1)} async-done(((bf16[4,48,1280]{2,1,0:T(8,128)(2,1)}), bf16[4,48,1280]{2,1,0:T(8,128)(2,1)S(1)}, u32[]{:S(2)}, u32[]{:S(2)}) %all-to-all-start.5) | async-done | bytes 491552 | tf_op jit(solution)/shard_map/all_to_all | solution.py:293
  44.9 3.5 all-to-all-start.9
  48.7 15.0 %all-to-all-done.9 = bf16[4,160,1024]{2,1,0:T(8,128)(2,1)S(1)} async-done(((bf16[4,160,1024]{2,1,0:T(8,128)(2,1)}), bf16[4,160,1024]{2,1,0:T(8,128)(2,1)S(1)}, u32[]{:S(2)}, u32[]{:S(2)}) %all-to-all-start.9) | async-done | bytes 1310752 | tf_op jit(solution)/shard_map/all_to_all | solution.py:293
  63.8 19.7 %all_to_all.63 = bf16[8,48,640]{2,1,0:T(8,128)(2,1)S(1)} all-to-all(bf16[8,48,640]{2,1,0:T(8,128)(2,1)S(1)} %bitcast.131), channel_id=1, replica_groups=mesh['rep'=8,'tp'=4] {'rep'}, dimensions={0} | all-to-all | bytes 983040 | tf_op jit(solution)/shard_map/all_to_all | solution.py:293
  83.4 1.4 broadcast_in_dim.168
  84.9 3.6 all-to-all-start.7
  88.5 11.8 %shard_map.140 = (f32[160,10240]{1,0:T(8,128)}, f32[160,10240]{1,0:T(8,128)}, f32[160,10240]{1,0:T(8,128)}, bf16[4,160,1536]{2,1,0:T(8,128)(2,1)}) custom-call(f32[160,10240]{1,0:T(8,128)} %master.2, f32[160,10240]{1,0:T(8,128)} %moment.2, f32[160,10240]{1,0:T(8,128)} %variance.2, ...), custom_call_target="tpu_custom_call", output_to_operand_aliasing={{0}: (4, {}), {1}: (5, {}), {2}: (6, {})} | custom-call | flops 14745600 | bytes 27525120 | tf_op jit(solution)/shard_map/pallas_call | solution.py:53
  100.2 11.6 %all-to-all-done.7 = bf16[4,8,48,640]{3,2,1,0:T(8,128)(2,1)S(1)} async-done(((bf16[4,8,48,640]{3,2,1,0:T(8,128)(2,1)}), bf16[4,8,48,640]{3,2,1,0:T(8,128)(2,1)S(1)}, u32[]{:S(2)}, u32[]{:S(2)}) %all-to-all-start.7) | async-done | bytes 1966112 | tf_op jit(solution)/shard_map/all_to_all | solution.py:293
  111.9 4.4 %all-to-all-start.8 = ((bf16[4,160,1536]{2,1,0:T(8,128)(2,1)}), bf16[4,160,1536]{2,1,0:T(8,128)(2,1)}, u32[]{:S(2)}, u32[]{:S(2)}) async-start(bf16[4,160,1536]{2,1,0:T(8,128)(2,1)} %get-tuple-element.206), calls=%async_computation.8 | async-start | bytes 3932160 | tf_op jit(solution)/shard_map/all_to_all | solution.py:293
  116.5 1.5 copy.38
  121.0 18.3 %all-to-all-done.8 = bf16[4,160,1536]{2,1,0:T(8,128)(2,1)} async-done(((bf16[4,160,1536]{2,1,0:T(8,128)(2,1)}), bf16[4,160,1536]{2,1,0:T(8,128)(2,1)}, u32[]{:S(2)}, u32[]{:S(2)}) %all-to-all-start.8) | async-done | bytes 1966112 | tf_op jit(solution)/shard_map/all_to_all | solution.py:293
  139.3 4.4 %fusion.60 = bf16[1,1024,640]{2,1,0:T(8,128)(2,1)S(1)} fusion(bf16[1536,640]{1,0:T(8,128)(2,1)} %bitcast.18, s32[1024]{0:T(1024)S(1)} %add_select_fusion.3), kind=kOutput, calls=%fused_computation.82 | convolution fusion | flops 2015494144 | bytes 3280896 | tf_op jit(solution)/shard_map/dot_general | solution.py:262
  143.7 2.8 fusion.59
  147.1 4.1 %fusion.62 = f32[1024,1536]{1,0:T(8,128)S(1)} fusion(bf16[640,1536]{1,0:T(8,128)(2,1)} %bitcast.23, bf16[2,1024,640]{2,1,0:T(8,128)(2,1)S(1)} %get-tuple-element.205), kind=kOutput, calls=%fused_computation.84 | convolution fusion | flops 2013265920 | bytes 9568256 | tf_op jit(solution)/shard_map/dot_general | solution.py:341
  151.2 4.2 %convolution_add_fusion = f32[1024,1536]{1,0:T(8,128)S(1)} fusion(f32[1024,1536]{1,0:T(8,128)S(1)} %fusion.62, bf16[640,1536]{1,0:T(8,128)(2,1)} %collective-permute-done.2, bf16[2,1024,640]{2,1,0:T(8,128)(2,1)S(1)} %get-tuple-element.205), kind=kOutput, calls=%fused_computation.38 | convolution fusion | flops 2014838784 | bytes 15859712 | tf_op jit(solution)/shard_map/dot_general | solution.py:341
  155.4 2.6 copy-done
  158.2 1.9 collective-permute-start.3
  160.8 33.8 %collective-permute-done.3 = bf16[256,1536]{1,0:T(8,128)(2,1)S(1)} collective-permute-done((bf16[256,1536]{1,0:T(8,128)(2,1)S(1)}, bf16[256,1536]{1,0:T(8,128)(2,1)S(1)}, u32[]{:S(2)}, u32[]{:S(2)}) %collective-permute-start.3) | collective-permute-done | bytes 786464 | tf_op jit(solution)/shard_map/ppermute | solution.py:222
  194.5 1.6 fusion.55
  196.2 4.7 %collective-permute-start.4 = (bf16[256,1536]{1,0:T(8,128)(2,1)S(1)}, bf16[256,1536]{1,0:T(8,128)(2,1)S(1)}, u32[]{:S(2)}, u32[]{:S(2)}) collective-permute-start(bf16[256,1536]{1,0:T(8,128)(2,1)S(1)} %fusion.55), channel_id=1, source_target_pairs={{0,8},{4,12},{8,16},{12,20},{1,9},{5,13},{9,17},{13,21},{2,10},{6,... | collective-permute-start | bytes 2359304 | tf_op jit(solution)/shard_map/ppermute | solution.py:222
  200.9 34.0 %collective-permute-done.4 = bf16[256,1536]{1,0:T(8,128)(2,1)S(1)} collective-permute-done((bf16[256,1536]{1,0:T(8,128)(2,1)S(1)}, bf16[256,1536]{1,0:T(8,128)(2,1)S(1)}, u32[]{:S(2)}, u32[]{:S(2)}) %collective-permute-start.4) | collective-permute-done | bytes 786464 | tf_op jit(solution)/shard_map/ppermute | solution.py:222
  234.8 3.2 fusion.56
  239.4 5.1 %collective-permute-start.5 = (bf16[256,1536]{1,0:T(8,128)(2,1)S(1)}, bf16[256,1536]{1,0:T(8,128)(2,1)S(1)}, u32[]{:S(2)}, u32[]{:S(2)}) collective-permute-start(bf16[256,1536]{1,0:T(8,128)(2,1)S(1)} %get-tuple-element.260), channel_id=1, source_target_pairs={{0,8},{4,12},{8,16},{12,20},{16,24},{20,28},{1,9},{5,13},{9,17},{1... | collective-permute-start | bytes 2359304 | tf_op jit(solution)/shard_map/ppermute | solution.py:222
  244.5 2.5 fusion.54
  247.0 1.3 collective-permute-start.8
  250.6 12.5 %shard_map.141 = bf16[384,1280]{1,0:T(8,128)(2,1)} custom-call(s32[384]{0:T(512)} %reshape.354.ids, bf16[9600,1280]{1,0:T(8,128)(2,1)} %get-tuple-element.579), custom_call_target="tpu_custom_call" | custom-call | bytes 19660800 | tf_op jit(solution)/shard_map/pallas_call | solution.py:115
  263.1 2.2 collective-permute-done.5
  265.3 16.4 %collective-permute-done.8 = bf16[256,1536]{1,0:T(8,128)(2,1)S(1)} collective-permute-done((bf16[256,1536]{1,0:T(8,128)(2,1)}, bf16[256,1536]{1,0:T(8,128)(2,1)S(1)}, u32[]{:S(2)}, u32[]{:S(2)}) %collective-permute-start.8) | collective-permute-done | bytes 786464 | tf_op jit(solution)/shard_map/ppermute | solution.py:222
  281.7 1.7 fusion.58
  283.9 3.6 all-to-all-start.4
  290.5 12.2 %shard_map.142 = bf16[64,2,16,128]{3,2,1,0:T(8,128)(2,1)} custom-call(s32[64]{0:T(128)} %lengths.1, bf16[64,2,16,128]{3,2,1,0:T(8,128)(2,1)} %reshape.366.queries, bf16[64,2,16,128]{3,2,1,0:T(8,128)(2,1)} %pad.7.fresh_keys, bf16[64,2,16,128]{3,2,1,0:T(8,128)(2,1)} %pad.8.fresh_values, bf16[64,192,256]{2,1,0:T(8,128)(2,1)} %keys.1, bf16[64,192,256]{2,1,0:T(8,128)(2,1)} %values.1), custom_call_target="tpu_custom_call" | custom-call | flops 201326592 | bytes 12582912 | tf_op jit(solution)/shard_map/pallas_call | solution.py:195
  302.7 1.2 reshape.367
  304.5 2.6 fusion.38
  307.1 2.6 fusion.41
  309.7 2.6 fusion.44
  312.4 2.6 fusion.47
  315.0 1.8 pad_maximum_fusion.2
  316.8 4.5 %all-to-all-start.10 = ((bf16[4,256,1280]{2,1,0:T(8,128)(2,1)}), bf16[4,256,1280]{2,1,0:T(8,128)(2,1)}, u32[]{:S(2)}, u32[]{:S(2)}) async-start(bf16[4,256,1280]{2,1,0:T(8,128)(2,1)} %pad_maximum_fusion.2), calls=%async_computation.10 | async-start | bytes 5242880 | tf_op jit(solution)/shard_map/all_to_all | solution.py:293
  323.8 29.0 %all-to-all-done.10 = bf16[4,256,1280]{2,1,0:T(8,128)(2,1)} async-done(((bf16[4,256,1280]{2,1,0:T(8,128)(2,1)}), bf16[4,256,1280]{2,1,0:T(8,128)(2,1)}, u32[]{:S(2)}, u32[]{:S(2)}) %all-to-all-start.10) | async-done | bytes 2621472 | tf_op jit(solution)/shard_map/all_to_all | solution.py:293
  352.7 2.2 convert_reduce_fusion.1
  355.3 1.5 collective-permute-start.11
  356.7 1.5 collective-permute-start.10
  360.3 1.5 collective-permute-done.9
  (77 shorter events, 16.6 us)
Async XLA Ops:
  7.2 9.3 %copy-start.5 = (s32[512,4]{0,1:T(4,128)S(1)}, s32[512,4]{0,1:T(4,128)}, u32[]{:S(2)}) copy-start(s32[512,4]{0,1:T(4,128)} %param.25) | copy-start | bytes 24580
  16.6 15.5 %copy-start.2 = (s32[512,4]{1,0:T(8,128)}, s32[512,4]{1,0:T(8,128)S(1)}, u32[]{:S(2)}) copy-start(s32[512,4]{1,0:T(8,128)S(1)} %copy.34) | copy-start | bytes 24580
  25.4 11.9 %copy-start.4 = (f32[5120]{0:T(1024)S(1)}, f32[5120]{0:T(1024)}, u32[]{:S(2)}) copy-start(f32[5120]{0:T(1024)} %param.20) | copy-start | bytes 61444
  32.1 12.6 %all-to-all-start.5 = ((bf16[4,48,1280]{2,1,0:T(8,128)(2,1)}), bf16[4,48,1280]{2,1,0:T(8,128)(2,1)S(1)}, u32[]{:S(2)}, u32[]{:S(2)}) async-start(bf16[4,48,1280]{2,1,0:T(8,128)(2,1)} %bitcast.132), calls=%async_computation.5 | async-start | bytes 983040 | tf_op jit(solution)/shard_map/all_to_all | solution.py:293
  44.9 18.9 %all-to-all-start.9 = ((bf16[4,160,1024]{2,1,0:T(8,128)(2,1)}), bf16[4,160,1024]{2,1,0:T(8,128)(2,1)S(1)}, u32[]{:S(2)}, u32[]{:S(2)}) async-start(bf16[4,160,1024]{2,1,0:T(8,128)(2,1)} %get-tuple-element.207), calls=%async_computation.9 | async-start | bytes 2621440 | tf_op jit(solution)/shard_map/all_to_all | solution.py:293
  63.8 21.1 %copy-start.1 = (bf16[4,160,1024]{2,1,0:T(8,128)(2,1)}, bf16[4,160,1024]{2,1,0:T(8,128)(2,1)S(1)}, u32[]{:S(2)}) copy-start(bf16[4,160,1024]{2,1,0:T(8,128)(2,1)S(1)} %all-to-all-done.9) | copy-start | bytes 3932164
  84.9 27.0 %all-to-all-start.7 = ((bf16[4,8,48,640]{3,2,1,0:T(8,128)(2,1)}), bf16[4,8,48,640]{3,2,1,0:T(8,128)(2,1)S(1)}, u32[]{:S(2)}, u32[]{:S(2)}) async-start(bf16[4,8,48,640]{3,2,1,0:T(8,128)(2,1)} %broadcast_in_dim.168), calls=%async_computation.7 | async-start | bytes 3932160 | tf_op jit(solution)/shard_map/all_to_all | solution.py:293
  111.9 27.4 %all-to-all-start.8 = ((bf16[4,160,1536]{2,1,0:T(8,128)(2,1)}), bf16[4,160,1536]{2,1,0:T(8,128)(2,1)}, u32[]{:S(2)}, u32[]{:S(2)}) async-start(bf16[4,160,1536]{2,1,0:T(8,128)(2,1)} %get-tuple-element.206), calls=%async_computation.8 | async-start | bytes 3932160 | tf_op jit(solution)/shard_map/all_to_all | solution.py:293
  116.3 188.1 %all-gather.2.cloned.1.call-start = ((), (), s32[]{:S(2)}) async-start(), calls=%async_computation.11 | async-start | bytes 11796480 | tf_op jit(solution)/shard_map/all_gather | solution.py:300
  118.0 25.7 %collective-permute-start.1 = (bf16[1536,640]{1,0:T(8,128)(2,1)}, bf16[1536,640]{1,0:T(8,128)(2,1)S(1)}, u32[]{:S(2)}, u32[]{:S(2)}) collective-permute-start(bf16[1536,640]{1,0:T(8,128)(2,1)} %bitcast.18), channel_id=1, source_target_pairs={{0,4},{4,0},{8,12},{12,8},{16,20},{20,16},{24,28},{28,24},{1,5},{5... | collective-permute-start | bytes 5898248 | tf_op jit(solution)/shard_map/ppermute | solution.py:217
  139.3 11.9 %collective-permute-start.2 = (bf16[640,1536]{1,0:T(8,128)(2,1)}, bf16[640,1536]{1,0:T(8,128)(2,1)}, u32[]{:S(2)}, u32[]{:S(2)}) collective-permute-start(bf16[640,1536]{1,0:T(8,128)(2,1)} %bitcast.23), channel_id=1, source_target_pairs={{0,4},{4,0},{8,12},{12,8},{16,20},{20,16},{24,28},{28,24},{1,5},{5... | collective-permute-start | bytes 5898248 | tf_op jit(solution)/shard_map/ppermute | solution.py:217
  155.4 2.6 copy-start
  158.2 36.4 %collective-permute-start.3 = (bf16[256,1536]{1,0:T(8,128)(2,1)S(1)}, bf16[256,1536]{1,0:T(8,128)(2,1)S(1)}, u32[]{:S(2)}, u32[]{:S(2)}) collective-permute-start(bf16[256,1536]{1,0:T(8,128)(2,1)S(1)} %get-tuple-element.262), channel_id=1, source_target_pairs={{0,8},{4,12},{1,9},{5,13},{2,10},{6,14},{3,11},{7,15}} | collective-permute-start | bytes 2359304 | tf_op jit(solution)/shard_map/ppermute | solution.py:222
  160.0 40.8 %collective-permute-start.6 = (bf16[256,1536]{1,0:T(8,128)(2,1)S(1)}, bf16[256,1536]{1,0:T(8,128)(2,1)S(1)}, u32[]{:S(2)}, u32[]{:S(2)}) collective-permute-start(bf16[256,1536]{1,0:T(8,128)(2,1)S(1)} %get-tuple-element.263), channel_id=1, source_target_pairs={{24,16},{28,20},{25,17},{29,21},{26,18},{30,22},{27,19},{31,23}} | collective-permute-start | bytes 2359304 | tf_op jit(solution)/shard_map/ppermute | solution.py:222
  196.2 38.7 %collective-permute-start.4 = (bf16[256,1536]{1,0:T(8,128)(2,1)S(1)}, bf16[256,1536]{1,0:T(8,128)(2,1)S(1)}, u32[]{:S(2)}, u32[]{:S(2)}) collective-permute-start(bf16[256,1536]{1,0:T(8,128)(2,1)S(1)} %fusion.55), channel_id=1, source_target_pairs={{0,8},{4,12},{8,16},{12,20},{1,9},{5,13},{9,17},{13,21},{2,10},{6,... | collective-permute-start | bytes 2359304 | tf_op jit(solution)/shard_map/ppermute | solution.py:222
  200.8 37.9 %copy-start.3 = (s32[512,4]{1,0:T(8,128)S(1)}, s32[512,4]{1,0:T(8,128)}, u32[]{:S(2)}) copy-start(s32[512,4]{1,0:T(8,128)} %copy-done.2) | copy-start | bytes 24580
  238.1 6.4 %collective-permute-start.7 = (bf16[256,1536]{1,0:T(8,128)(2,1)}, bf16[256,1536]{1,0:T(8,128)(2,1)S(1)}, u32[]{:S(2)}, u32[]{:S(2)}) collective-permute-start(bf16[256,1536]{1,0:T(8,128)(2,1)} %get-tuple-element.261), channel_id=1, source_target_pairs={{16,8},{20,12},{24,16},{28,20},{17,9},{21,13},{25,17},{29,21},{18,... | collective-permute-start | bytes 2359304 | tf_op jit(solution)/shard_map/ppermute | solution.py:222
  239.4 25.9 %collective-permute-start.5 = (bf16[256,1536]{1,0:T(8,128)(2,1)S(1)}, bf16[256,1536]{1,0:T(8,128)(2,1)S(1)}, u32[]{:S(2)}, u32[]{:S(2)}) collective-permute-start(bf16[256,1536]{1,0:T(8,128)(2,1)S(1)} %get-tuple-element.260), channel_id=1, source_target_pairs={{0,8},{4,12},{8,16},{12,20},{16,24},{20,28},{1,9},{5,13},{9,17},{1... | collective-permute-start | bytes 2359304 | tf_op jit(solution)/shard_map/ppermute | solution.py:222
  247.0 34.7 %collective-permute-start.8 = (bf16[256,1536]{1,0:T(8,128)(2,1)}, bf16[256,1536]{1,0:T(8,128)(2,1)S(1)}, u32[]{:S(2)}, u32[]{:S(2)}) collective-permute-start(bf16[256,1536]{1,0:T(8,128)(2,1)} %fusion.54), channel_id=1, source_target_pairs={{8,0},{12,4},{16,8},{20,12},{24,16},{28,20},{9,1},{13,5},{17,9},{2... | collective-permute-start | bytes 2359304 | tf_op jit(solution)/shard_map/ppermute | solution.py:222
  283.9 32.9 %all-to-all-start.4 = ((bf16[8,48,1280]{2,1,0:T(8,128)(2,1)}), bf16[8,48,1280]{2,1,0:T(8,128)(2,1)S(1)}, u32[]{:S(2)}, u32[]{:S(2)}) async-start(bf16[8,48,1280]{2,1,0:T(8,128)(2,1)} %bitcast.11), calls=%async_computation.4 | async-start | bytes 1966080 | tf_op jit(solution)/shard_map/all_to_all | solution.py:293
  316.8 36.0 %all-to-all-start.10 = ((bf16[4,256,1280]{2,1,0:T(8,128)(2,1)}), bf16[4,256,1280]{2,1,0:T(8,128)(2,1)}, u32[]{:S(2)}, u32[]{:S(2)}) async-start(bf16[4,256,1280]{2,1,0:T(8,128)(2,1)} %pad_maximum_fusion.2), calls=%async_computation.10 | async-start | bytes 5242880 | tf_op jit(solution)/shard_map/all_to_all | solution.py:293
  355.3 4.5 %collective-permute-start.11 = (f32[256]{0:T(256)S(1)}, f32[256]{0:T(256)S(1)}, u32[]{:S(2)}, u32[]{:S(2)}) collective-permute-start(f32[256]{0:T(256)S(1)} %multiply_reduce_fusion), channel_id=1, source_target_pairs={{0,3},{1,2},{2,1},{3,0},{4,7},{5,6},{6,5},{7,4},{8,11},{9,10},{10,... | collective-permute-start | bytes 3080 | tf_op jit(solution)/shard_map/ppermute | solution.py:217
  356.7 3.6 collective-permute-start.10
  358.2 3.6 collective-permute-start.9
Sparse Core Ops, SparseCore 0:
  121.1 131.7 all-gather.1
where the time goes:
time: 377 us; the launch traced here: 370 us
  waiting for transfers between devices  170 us (45%)
  Pallas kernels  52.3 us (14%)
  starting transfers between devices  42.9 us (11%)
  matrix products  26.6 us (7%)
  other arithmetic  25 us (7%)
  blocking collectives  19.7 us (5%)
  between operations  19 us (5%)
  local copies, waits for them, and re-layouts  14.6 us (4%)
    ppermute x6, waiting for transfers between devices, hop(): return lax.ppermute(values, 'rep', pairs)  86.3 us
    all_to_all x6, waiting for transfers between devices, shards(): lax.all_to_all(values, axis, split_axis=0, concat_axis=0, tiled=True)  81.3 us
    all_to_all x6, starting transfers between devices, shards(): lax.all_to_all(values, axis, split_axis=0, concat_axis=0, tiled=True)  24.9 us
    pallas_call x2, Pallas kernels, adam(): pl.pallas_call(adam_body, grid=(groups,), in_specs=[part] * 4 + [pl.Block...  21 us
    all_to_all x1, blocking collectives, shards(): lax.all_to_all(values, axis, split_axis=0, concat_axis=0, tiled=True)  19.7 us
    pallas_call x2, Pallas kernels, gather_rows(): pl.pallas_call(gather_body, grid_spec=pltpu.PrefetchScalarGridSpec(num_sc...  19.1 us
    ppermute x6, starting transfers between devices, hop(): return lax.ppermute(values, 'rep', pairs)  14.3 us
    pallas_call x1, Pallas kernels, attend(): pl.pallas_call(functools.partial(attend_body, block_row=block_row), grid_...  12.2 us
  transfers between devices with their start and end apart: 18, of which 12 were waited for; matrix products, arithmetic and copies ran while one was open for 13% of the time, Pallas kernels for 10%

commit v1 on v0

--- a/solution.py
+++ b/solution.py
@@ -16,6 +16,8 @@
 OUTER = QG * HEAD_SIZE
 SLOTS = 192
 ROW_SLOTS = 48
+PROJECT_STEPS = 2
+ATTEND_ROWS = 8
 
 
 beta_one = 0.9
@@ -134,82 +136,83 @@
     )(ids, embed)
 
 
-def attend_body(lengths, queries, fresh_keys, fresh_values, keys, values, heads, *, block_row):
-    rows, groups, lines, width = queries.shape
-    places = keys.shape[1]
+def attend_body(lengths, fresh, keys, values, heads):
+    rows, groups, _, width = fresh.shape
+    lines, places = QG * STEPS, keys.shape[1]
     scale = width ** (-0.5)
-    start = block_row(pl.program_id(0)) * rows
+    start = pl.program_id(0) * rows
     column = lax.broadcasted_iota(jnp.int32, (lines, places), 1)
-    step_of = lax.broadcasted_iota(jnp.int32, (lines, lines), 0) // QG
-    causal = lax.broadcasted_iota(jnp.int32, (lines, lines), 1) <= step_of
+    step_of = lax.broadcasted_iota(jnp.int32, (lines, 2 * STEPS), 0) % STEPS
+    turn = lax.broadcasted_iota(jnp.int32, (lines, 2 * STEPS), 1) - STEPS
+    causal = (turn >= 0) & (turn <= step_of)
     across = (((1,), (1,)), ((), ()))
     scores = []
     for row in range(rows):
         live = column < lengths[start + row]
         for group in range(groups):
             at = slice(group * width, (group + 1) * width)
-            query = queries[row, group]
+            query = fresh[row, group, :lines]
+            both = fresh[row, group, lines:]
+            turned = pltpu.roll(both.astype(jnp.float32), STEPS, axis=0).astype(jnp.bfloat16)
             cached = lax.dot_general(
                 query, keys[row, :, at], across, preferred_element_type=jnp.float32
             )
-            fresh = lax.dot_general(
-                query, fresh_keys[row, group], across, preferred_element_type=jnp.float32
-            )
+            new = lax.dot_general(query, turned, across, preferred_element_type=jnp.float32)
             cached = jnp.where(live, cached * scale, masked_score)
-            fresh = jnp.where(causal, fresh * scale, masked_score)
-            scores.append((cached, fresh))
+            new = jnp.where(causal, new * scale, masked_score)
+            scores.append((cached, new, both))
     probs = []
-    for cached, fresh in scores:
+    for cached, new, both in scores:
         top = jnp.maximum(
-            jnp.max(cached, axis=-1, keepdims=True), jnp.max(fresh, axis=-1, keepdims=True)
+            jnp.max(cached, axis=-1, keepdims=True), jnp.max(new, axis=-1, keepdims=True)
         )
         cached = jnp.exp(cached - top)
-        fresh = jnp.exp(fresh - top)
-        total = jnp.sum(cached, axis=-1, keepdims=True) + jnp.sum(fresh, axis=-1, keepdims=True)
-        probs.append(((cached / total).astype(jnp.bfloat16), (fresh / total).astype(jnp.bfloat16)))
+        new = jnp.exp(new - top)
+        total = jnp.sum(cached, axis=-1, keepdims=True) + jnp.sum(new, axis=-1, keepdims=True)
+        probs.append(
+            ((cached / total).astype(jnp.bfloat16), (new / total).astype(jnp.bfloat16), both)
+        )
     for row in range(rows):
         for group in range(groups):
             at = slice(group * width, (group + 1) * width)
-            cached, fresh = probs[row * groups + group]
+            cached, new, both = probs[row * groups + group]
             out = jnp.dot(cached, values[row, :, at], preferred_element_type=jnp.float32)
-            out = out + jnp.dot(
-                fresh, fresh_values[row, group], preferred_element_type=jnp.float32
-            )
+            out = out + jnp.dot(new, both, preferred_element_type=jnp.float32)
             heads[row, group] = out.astype(jnp.bfloat16)
 
 
-def attend(projected, keys, values, lengths, rows, chunk, chunks):
+def attend(projected, keys, values, lengths):
     count, columns = projected.shape
     groups = columns // INNER
     here = count // STEPS
+    rows = min(ATTEND_ROWS, here)
     lines = STEPS * QG
-    split = projected.reshape(here, STEPS, groups, INNER).transpose(0, 2, 1, 3)
-    queries = split[..., :OUTER].reshape(here, groups, lines, HEAD_SIZE)
-    pad = ((0, 0), (0, 0), (0, lines - STEPS), (0, 0))
-    fresh_keys = jnp.pad(split[..., OUTER : OUTER + HEAD_SIZE], pad)
-    fresh_values = jnp.pad(split[..., OUTER + HEAD_SIZE :], pad)
+    fresh = projected.reshape(here, STEPS, groups, QG + 2, HEAD_SIZE).transpose(0, 2, 3, 1, 4)
+    fresh = fresh.reshape(here, groups, lines + 2 * STEPS, HEAD_SIZE)
     places, width = keys.shape[1:]
-    block_row = lambda i: i * chunks + chunk
-    small = pl.BlockSpec((rows, groups, lines, HEAD_SIZE), lambda i, _: (i, 0, 0, 0))
-    cache = pl.BlockSpec((rows, places, width), lambda i, _: (block_row(i), 0, 0))
+    cache = pl.BlockSpec((rows, places, width), lambda i, _: (i, 0, 0))
     heads = pl.pallas_call(
-        functools.partial(attend_body, block_row=block_row),
+        attend_body,
         grid_spec=pltpu.PrefetchScalarGridSpec(
             num_scalar_prefetch=1,
             grid=(here // rows,),
-            in_specs=[small, small, small, cache, cache],
-            out_specs=small,
-        ),
-        out_shape=jax.ShapeDtypeStruct(queries.shape, jnp.bfloat16),
+            in_specs=[
+                pl.BlockSpec((rows,) + fresh.shape[1:], lambda i, _: (i, 0, 0, 0)),
+                cache,
+                cache,
+            ],
+            out_specs=pl.BlockSpec((rows, groups, lines, HEAD_SIZE), lambda i, _: (i, 0, 0, 0)),
+        ),
+        out_shape=jax.ShapeDtypeStruct((here, groups, lines, HEAD_SIZE), jnp.bfloat16),
         compiler_params=pltpu.CompilerParams(vmem_limit_bytes=56 * 2**20),
         cost_estimate=pl.CostEstimate(
             flops=4 * here * groups * lines * places * HEAD_SIZE,
             bytes_accessed=4 * here * places * width,
             transcendentals=here * groups * lines * places,
         ),
-    )(lengths, queries, fresh_keys, fresh_values, keys, values)
-    heads = heads.reshape(here, groups, STEPS, OUTER).transpose(0, 2, 1, 3)
-    return heads.reshape(count, groups * OUTER)
+    )(lengths, fresh, keys, values)
+    heads = heads.reshape(here, groups, QG, STEPS, HEAD_SIZE).transpose(1, 2, 4, 0, 3)
+    return heads.reshape(groups * OUTER, count)
 
 
 def flip(values, axis, bit):
@@ -226,7 +229,70 @@
     return lax.dynamic_index_in_dim(values, index, 0, keepdims=False)
 
 
-def line_sum(block, plane, planes):
+def outward_body(weights, heads, out):
+    found = jnp.dot(weights[...], heads[...], preferred_element_type=jnp.float32)
+    out[0] = found.astype(out.dtype)
+
+
+def outward(weights, heads, n_tp):
+    depth, count = heads.shape
+    width = weights.shape[0] // n_tp
+    return pl.pallas_call(
+        outward_body,
+        grid=(n_tp,),
+        in_specs=[
+            pl.BlockSpec((width, depth), lambda i: (i, 0)),
+            pl.BlockSpec((depth, count), lambda i: (0, 0)),
+        ],
+        out_specs=pl.BlockSpec((1, width, count), lambda i: (i, 0, 0)),
+        out_shape=jax.ShapeDtypeStruct((n_tp, width, count), jnp.bfloat16),
+        compiler_params=pltpu.CompilerParams(vmem_limit_bytes=56 * 2**20),
+        cost_estimate=pl.CostEstimate(
+            flops=2 * count * depth * width * n_tp,
+            bytes_accessed=2 * depth * width * n_tp,
+            transcendentals=0,
+        ),
+    )(weights, heads)
+
+
+def project_body(slots, here, there, inner_here, inner_there, out):
+    rows = here.shape[0]
+    column = lax.broadcasted_iota(jnp.int32, (slots.shape[0], rows), 1)
+    pick = (column == slots[...]).astype(jnp.bfloat16)
+    dot = functools.partial(jnp.dot, preferred_element_type=jnp.float32)
+    first = dot(pick, here[...]).astype(jnp.bfloat16)
+    second = dot(pick, there[...]).astype(jnp.bfloat16)
+    out[...] = dot(first, inner_here[...]) + dot(second, inner_there[...])
+
+
+def project(slots, here, there, inner_here, inner_there, planes):
+    total = slots.shape[0]
+    count = total // PROJECT_STEPS
+    rows, depth = here.shape
+    columns = inner_here.shape[1]
+    all_of = lambda shape: pl.BlockSpec(shape, lambda i: (0, 0))
+    return pl.pallas_call(
+        project_body,
+        grid=(PROJECT_STEPS,),
+        in_specs=[pl.BlockSpec((count, 1), lambda i: (i, 0))]
+        + [all_of((rows, depth))] * 2
+        + [all_of((depth, columns))] * 2,
+        out_specs=pl.BlockSpec((count, columns), lambda i: (i, 0)),
+        out_shape=jax.ShapeDtypeStruct((total, columns), jnp.float32),
+        compiler_params=pltpu.CompilerParams(vmem_limit_bytes=56 * 2**20),
+        cost_estimate=pl.CostEstimate(
+            flops=4 * total * depth * (rows + columns),
+            bytes_accessed=4 * (rows + columns) * depth + 4 * total * columns,
+            transcendentals=0,
+        ),
+    )(slots, here, there, inner_here, inner_there).reshape(planes, -1, columns)
+
+
+def tie(values, *others):
+    return lax.optimization_barrier((values, others))
+
+
+def line_sum(block, plane, planes, late):
     right = left = None
     for step in range(1, planes):
         forth = block(jnp.minimum(plane + planes - step, planes - 1))
@@ -235,37 +301,51 @@
             forth, back = forth + right, back + left
         right = hop(forth.astype(jnp.bfloat16), 0, step, 1)
         left = hop(back.astype(jnp.bfloat16), planes - step, planes, -1)
-    return block(plane) + right.astype(jnp.float32) + left.astype(jnp.float32)
-
-
-def numbers(ids, block):
+        if step == max(planes - 2, 1):
+            (right, left), (late,) = tie((right, left), late)
+    return block(plane) + right.astype(jnp.float32) + left.astype(jnp.float32), late
+
+
+def leaders(ids):
     count = ids.shape[-1]
     index = jnp.arange(count, dtype=jnp.int32)
     same = ids[..., :, None] == ids[..., None, :]
     leader = jnp.min(jnp.where(same, index[:, None], count), axis=-2)
-    first = leader == index
+    return leader, leader == index
+
+
+def numbers(block, leader, first):
+    index = jnp.arange(block.shape[-1], dtype=jnp.int32)
     ahead = (block[..., :, None] == block[..., None, :]) & first[..., :, None]
     ahead = ahead & (index[:, None] < leader[..., None, :])
-    return first, jnp.sum(ahead.astype(jnp.int32), axis=-2)
-
-
-def listed(ids, chosen, number, low, slots):
+    return jnp.sum(ahead.astype(jnp.int32), axis=-2)
+
+
+def listed(values, chosen, number, low, slots):
     at = jnp.where(chosen, number - low, -1)
     hit = at[..., :, None] == jnp.arange(slots, dtype=jnp.int32)
-    return jnp.sum(jnp.where(hit, ids[..., :, None], 0), axis=-2)
-
-
-def placed(rows, block, number, low, slots):
+    return jnp.sum(jnp.where(hit, values[..., :, None], 0), axis=-2)
+
+
+def slot_of(block, number, low, slots):
     slot = number - low
-    at = jnp.where((slot >= 0) & (slot < slots), block * slots + slot, -1)
-    pick = at[:, None] == jnp.arange(rows.shape[0], dtype=jnp.int32)[None, :]
+    return jnp.where((slot >= 0) & (slot < slots), block * slots + slot, -1)
+
+
+def picked(slot, rows):
+    pick = slot[:, None] == jnp.arange(rows.shape[0], dtype=jnp.int32)[None, :]
     return jnp.dot(pick.astype(jnp.bfloat16), rows, preferred_element_type=jnp.float32).astype(
         jnp.bfloat16
     )
 
 
-def in_rounds(rounds, one_round):
-    return lax.fori_loop(1, rounds, lambda turn, kept: kept + one_round(turn), one_round(0))
+def exchange(blocks, axis, place):
+    n = blocks.shape[0]
+    out = lax.dynamic_update_index_in_dim(blocks, block_of(blocks, place), place, 0)
+    for mask in range(1, n):
+        got = flip(block_of(blocks, place ^ mask), axis, mask)
+        out = lax.dynamic_update_index_in_dim(out, got, place ^ mask, 0)
+    return out
 
 
 def shards(
@@ -294,83 +374,105 @@
         values, axis, split_axis=0, concat_axis=0, tiled=True
     )
 
-    weights_in = (master, first_moment, second_moment, grads)
-    *partial, outer = adam(weights_in, (), n_tp, INNER, OUTER)
-    outer = swap(outer).reshape(depth, -1)
-    out_weights = lax.all_gather(outer, "rep", axis=0, tiled=True)
-
-    token_ids, _ = lax.optimization_barrier((token_ids, partial[0]))
     ids = token_ids.reshape(n_rep, count)
     block = ids // vocab_local
     flat_ids, flat_block = ids.reshape(-1), block.reshape(-1)
-    first, number = numbers(flat_ids, flat_block)
-    core_tokens = lambda values: lax.dynamic_index_in_dim(
-        values.reshape(planes, 2, count), core, 1, keepdims=False
-    ).reshape(-1)
-    core_block, core_number = core_tokens(flat_block), core_tokens(number)
+    leader, first = leaders(flat_ids)
+    mine = first & (flat_block == rep)
+    index = jnp.arange(flat_ids.shape[0], dtype=jnp.int32)
+    place = jnp.sum((mine[:, None] & (index[:, None] < index[None, :])).astype(jnp.int32), axis=0)
     local_ids = flat_ids - rep * vocab_local
-
-    def fetch(turn):
-        return gather_rows(
-            embed, listed(local_ids, first & (flat_block == rep), number, turn * SLOTS, SLOTS)
-        )
-
+    fetch = lambda turn: gather_rows(embed, listed(local_ids, mine, place, turn * SLOTS, SLOTS))
     rows = fetch(0)
-    held = lax.optimization_barrier((*weights_in, *partial, rows))
-    updated, new_first, second, inner = adam(held[:4], held[4:7], n_tp, 0, INNER)
-    inner = swap(inner).reshape(depth, -1)
-    inner_other = flip(inner, "rep", 1)
-
-    def normed_rows(turn):
-        found = rows if isinstance(turn, int) else fetch(turn)
-        tokens = swap(found.reshape(n_tp, -1, width_local)).astype(jnp.float32)
+    swapped = swap(rows.reshape(n_tp, -1, width_local))
+
+    weights_in = (master, first_moment, second_moment, grads)
+    weights_in, _ = tie(weights_in, rows)
+    *partial, outer = adam(weights_in, (), n_tp, INNER, OUTER)
+    swapped, (outer,) = tie(swapped, outer)
+    outer = exchange(outer, "tp", tp).reshape(depth, -1)
+    out_weights = lax.all_gather(outer, "rep", axis=0, tiled=True)
+
+    def normed_rows(found):
+        tokens = found.astype(jnp.float32)
         mean_sq = jnp.sum(tokens * tokens, axis=(0, 2), keepdims=True) / MODEL_WIDTH
         normed_in = tokens * lax.rsqrt(mean_sq + norm_eps) * ln_gain.reshape(n_tp, 1, width_local)
         normed_in = normed_in.astype(jnp.bfloat16)
         share = normed_in.shape[1]
         normed_in = normed_in.reshape(n_tp, share, n_rep // n_tp, depth).transpose(0, 2, 1, 3)
-        got = swap(normed_in.reshape(n_rep, share, depth), "rep")
+        return normed_in.reshape(n_rep, share, depth)
+
+    def all_slots(got):
         got = swap(jnp.broadcast_to(got[None], (n_tp,) + got.shape))
-        got = got.transpose(1, 0, 2, 3).reshape(-1, depth)
-        other = flip(got, "rep", 1)
-        put = lambda values: placed(values, core_block, core_number, turn * SLOTS, SLOTS)
-        return jnp.stack([put(got), put(other)])
-
+        return got.transpose(1, 0, 2, 3).reshape(-1, depth)
+
+    normed_in = normed_rows(swapped)
+    got = swap(normed_in, "rep")
+    (weights_in, partial), _ = tie((weights_in, partial), normed_in)
+    updated, new_first, second, inner = adam(weights_in, partial, n_tp, 0, INNER)
+    got, (inner,) = tie(got, inner)
+    inner = exchange(inner, "tp", tp).reshape(depth, -1)
+    got, (inner,) = tie(got, inner)
+    inner_other = flip(inner, "rep", 1)
+
+    here = all_slots(got)
+    flat_block, _ = tie(flat_block, got)
+    number = numbers(flat_block, leader, first)
+    core_tokens = lambda values: lax.dynamic_index_in_dim(
+        values.reshape(planes, 2, count), core, 1, keepdims=False
+    ).reshape(-1)
+    core_block, core_number = core_tokens(flat_block), core_tokens(number)
     rounds = jnp.max(number) // SLOTS + 1
-    spread = in_rounds(rounds, normed_rows)
-    project = lambda x, w: jnp.dot(x, w, preferred_element_type=jnp.float32)
-    terms = project(spread[0], inner) + project(spread[1], inner_other)
-    terms = terms.reshape(planes, count, -1)
-    projected = line_sum(lambda d: block_of(terms, d), plane, planes).astype(jnp.bfloat16)
-
-    heads = attend(projected, cache_keys, stored_values, lengths, 8, 0, 1)
-
-    row_first, row_number = numbers(ids, block)
+
+    def terms_of(here, turn):
+        slot = slot_of(core_block, core_number, turn * SLOTS, SLOTS)
+        return project(slot[:, None], here, flip(here, "rep", 1), inner, inner_other, planes)
+
+    def terms_again(turn):
+        found = swap(fetch(turn).reshape(n_tp, -1, width_local))
+        return terms_of(all_slots(swap(normed_rows(found), "rep")), turn)
+
+    terms = terms_of(here, 0)
+    terms = lax.fori_loop(1, rounds, lambda turn, kept: kept + terms_again(turn), terms)
+
+    ids, _ = tie(ids, terms)
+    row_leader, row_first = leaders(ids)
+    row_number = numbers(block, row_leader, row_first)
     my_block, my_number = block_of(block, rep), block_of(row_number, rep)
 
-    def own_rows(turn):
-        low = turn * ROW_SLOTS
-        wanted = listed(
-            ids - rep * vocab_local, row_first & (block == rep), row_number, low, ROW_SLOTS
-        )
-        sent = gather_rows(embed, wanted.reshape(-1)).reshape(n_rep, ROW_SLOTS, width_local)
-        got = swap(sent, "rep").reshape(-1, width_local)
-        return placed(got, my_block, my_number, low, ROW_SLOTS)
-
-    own_cols = in_rounds(jnp.max(row_number) // ROW_SLOTS + 1, own_rows)
-
-    partial_out = jnp.stack(
-        [
-            lax.dot_general(
-                heads,
-                out_weights[at * width_local : (at + 1) * width_local],
-                (((1,), (1,)), ((), ())),
-                preferred_element_type=jnp.float32,
-            ).astype(jnp.bfloat16)
-            for at in range(n_tp)
-        ]
-    )
-    attended = jnp.sum(swap(partial_out).astype(jnp.float32), axis=0)
+    def to_send(far, near, found):
+        low = far * ROW_SLOTS
+        chosen = row_first & (block == rep)
+        of = listed(number.reshape(n_rep, -1) + 1, chosen, row_number, low, ROW_SLOTS)
+        slot = slot_of(0, of.reshape(-1) - 1, near * SLOTS, SLOTS)
+        return picked(slot, found).reshape(n_rep, ROW_SLOTS, width_local)
+
+    def own_rows(far, sent):
+        found = swap(sent, "rep").reshape(-1, width_local)
+        return picked(slot_of(my_block, my_number, far * ROW_SLOTS, ROW_SLOTS), found)
+
+    sent = to_send(0, 0, rows)
+    projected, (out_weights, sent) = line_sum(
+        lambda d: block_of(terms, d), plane, planes, (out_weights, sent)
+    )
+    projected = projected.astype(jnp.bfloat16)
+    sent, _ = tie(sent, projected)
+    own_cols = own_rows(0, sent)
+
+    heads = attend(projected, cache_keys, stored_values, lengths)
+    heads, (own_cols,) = tie(heads, own_cols)
+    own_cols = lax.fori_loop(
+        1,
+        (jnp.max(row_number) // ROW_SLOTS + 1) * rounds,
+        lambda turn, kept: kept
+        + own_rows(
+            turn // rounds, to_send(turn // rounds, turn % rounds, fetch(turn % rounds))
+        ),
+        own_cols,
+    )
+
+    partial_out = outward(out_weights, heads, n_tp)
+    attended = jnp.sum(swap(partial_out).astype(jnp.float32), axis=0).T
     resid = own_cols.astype(jnp.float32) + attended
     square = jnp.sum(resid * resid, axis=-1)
     total = functools.reduce(

time: 377 us -> 325 us (0.86); the launches traced: 370 us -> 324 us
  waiting for transfers between devices: 170 us -> 139 us
  matrix products: 26.6 us -> 1.96 us
  blocking collectives: 19.7 us -> 0 us
  starting transfers between devices: 42.9 us -> 54.2 us
  local copies, waits for them, and re-layouts: 14.6 us -> 25.2 us
  Pallas kernels: 52.3 us -> 61.9 us
    ppermute x6, waiting for transfers between devices: 86.3 us -> 57.9 us  [hop(): return lax.ppermute(values, 'rep', pairs)]
    dot_general x9 -> x2, matrix products: 26.6 us -> 1.96 us  [picked(): jnp.dot(pick.astype(jnp.bfloat16), rows, preferred_element_type=jnp.float32)]
    pallas_call x1 -> x3, Pallas kernels: 12.2 us -> 34.7 us  [the longest x1 15.2 us: project(): pl.pallas_call(project_body, grid=(PROJECT_STEPS,), in_specs=[pl.BlockSpe...]
    all_to_all x6 -> x5, waiting for transfers between devices: 81.3 us -> 60.2 us  [shards(): lax.all_to_all(values, axis, split_axis=0, concat_axis=0, tiled=True)]
    all_to_all x1 -> x0, blocking collectives: 19.7 us -> none  [shards(): lax.all_to_all(values, axis, split_axis=0, concat_axis=0, tiled=True)]
    ppermute x5 -> x11, waiting for transfers between devices: 2.19 us -> 20.9 us  [flip(): return lax.ppermute(values, axis, [(i, i ^ bit) for i in range(n)])]
    pallas_call x2 -> x1, Pallas kernels: 19.1 us -> 6.18 us  [gather_rows(): pl.pallas_call(gather_body, grid_spec=pltpu.PrefetchScalarGridSpec(num_sc...]
    ppermute x5 -> x11, starting transfers between devices: 3.55 us -> 10.7 us  [flip(): return lax.ppermute(values, axis, [(i, i ^ bit) for i in range(n)])]
  transfers between devices with their start and end apart: 18 -> 23, of which waited for: 12 -> 12; matrix products, arithmetic and copies ran while one was open for 13% -> 10% of each run, Pallas kernels for 10% -> 15%
where the time goes in v1:
time: 325 us; the launch traced here: 324 us
  waiting for transfers between devices  139 us (43%)
  Pallas kernels  61.9 us (19%)
  starting transfers between devices  54.2 us (17%)
  local copies, waits for them, and re-layouts  25.2 us (8%)
  other arithmetic  23.3 us (7%)
  between operations  18.4 us (6%)
    all_to_all x5, waiting for transfers between devices, shards(): lax.all_to_all(values, axis, split_axis=0, concat_axis=0, tiled=True)  60.2 us
    ppermute x6, waiting for transfers between devices, hop(): return lax.ppermute(values, 'rep', pairs)  57.9 us
    all_to_all x5, starting transfers between devices, shards(): lax.all_to_all(values, axis, split_axis=0, concat_axis=0, tiled=True)  23.9 us
    pallas_call x2, Pallas kernels, adam(): pl.pallas_call(adam_body, grid=(groups,), in_specs=[part] * 4 + [pl.Block...  21 us
    ppermute x11, waiting for transfers between devices, flip(): return lax.ppermute(values, axis, [(i, i ^ bit) for i in range(n)])  20.9 us
    ppermute x6, starting transfers between devices, hop(): return lax.ppermute(values, 'rep', pairs)  19.5 us
    pallas_call x1, Pallas kernels, project(): pl.pallas_call(project_body, grid=(PROJECT_STEPS,), in_specs=[pl.BlockSpe...  15.2 us
    pallas_call x1, Pallas kernels, attend(): pl.pallas_call(attend_body, grid_spec=pltpu.PrefetchScalarGridSpec(num_sc...  12 us
  transfers between devices with their start and end apart: 23, of which 12 were waited for; matrix products, arithmetic and copies ran while one was open for 10% of the time, Pallas kernels for 15%

profile of v1, /device:TPU:0, one launch (start us, length us, event | category | flops | bytes accessed | tf_op | source)
XLA Modules:
  0.0 323.9 jit_solution(2554525165876612854)
XLA Ops:
  8.2 2.3 select_reduce_fusion.3
  11.7 6.2 %shard_map.138 = bf16[192,1280]{1,0:T(8,128)(2,1)} custom-call(s32[192]{0:T(256)} %select_reduce_fusion.5.ids, bf16[9600,1280]{1,0:T(8,128)(2,1)} %embed.1), custom_call_target="tpu_custom_call" | custom-call | bytes 9830400 | tf_op jit(solution)/shard_map/pallas_call | solution.py:117
  17.9 5.2 %all-to-all-start.4 = ((bf16[4,48,1280]{2,1,0:T(8,128)(2,1)}), bf16[4,48,1280]{2,1,0:T(8,128)(2,1)S(1)}, u32[]{:S(2)}, u32[]{:S(2)}) async-start(bf16[4,48,1280]{2,1,0:T(8,128)(2,1)} %bitcast.128), calls=%async_computation.4 | async-start | bytes 983040 | tf_op jit(solution)/shard_map/all_to_all | solution.py:373
  23.1 9.2 %shard_map.139 = (f32[160,10240]{1,0:T(8,128)}, f32[160,10240]{1,0:T(8,128)}, f32[160,10240]{1,0:T(8,128)}, bf16[4,160,1024]{2,1,0:T(8,128)(2,1)}) custom-call(f32[160,10240]{1,0:T(8,128)} %master.1, f32[160,10240]{1,0:T(8,128)} %moment.1, f32[160,10240]{1,0:T(8,128)} %variance.1, bf16[160,10240]{1,0:T(8,128)(2,1)} %grads.1), custom_call_target="tpu_custom_call" | custom-call | flops 9830400 | bytes 18350080 | tf_op jit(solution)/shard_map/pallas_call | solution.py:55
  33.6 5.6 %all-to-all-start.5 = ((bf16[8,48,640]{2,1,0:T(8,128)(2,1)}), bf16[8,48,640]{2,1,0:T(8,128)(2,1)S(1)}, u32[]{:S(2)}, u32[]{:S(2)}) async-start(bf16[8,48,640]{2,1,0:T(8,128)(2,1)} %bitcast.9), calls=%async_computation.5 | async-start | bytes 983040 | tf_op jit(solution)/shard_map/all_to_all | solution.py:373
  40.1 2.0 collective-permute-start.10
  42.1 1.5 collective-permute-start.11
  43.6 11.8 %shard_map.140 = (f32[160,10240]{1,0:T(8,128)}, f32[160,10240]{1,0:T(8,128)}, f32[160,10240]{1,0:T(8,128)}, bf16[4,160,1536]{2,1,0:T(8,128)(2,1)}) custom-call(f32[160,10240]{1,0:T(8,128)} %master.1, f32[160,10240]{1,0:T(8,128)} %moment.1, f32[160,10240]{1,0:T(8,128)} %variance.1, ...), custom_call_target="tpu_custom_call", output_to_operand_aliasing={{0}: (4, {}), {1}: (5, {}), {2}: (6, {})} | custom-call | flops 14745600 | bytes 27525120 | tf_op jit(solution)/shard_map/pallas_call | solution.py:55
  55.4 2.8 dynamic-slice_bitcast_fusion
  58.2 2.0 collective-permute-start.1
  61.2 1.0 bitcast_dynamic-update-slice_fusion.4
  62.2 1.5 collective-permute-start.2
  63.7 1.0 bitcast_dynamic-update-slice_fusion.3
  64.7 1.0 copy-done.3
  65.9 6.6 %collective-permute-done.1 = bf16[160,1536]{1,0:T(8,128)(2,1)S(1)} collective-permute-done((bf16[160,1536]{1,0:T(8,128)(2,1)}, bf16[160,1536]{1,0:T(8,128)(2,1)S(1)}, u32[]{:S(2)}, u32[]{:S(2)}) %collective-permute-start.1) | collective-permute-done | bytes 491552 | tf_op jit(solution)/shard_map/ppermute | solution.py:220
  73.4 12.1 %collective-permute-done.2 = bf16[160,1536]{1,0:T(8,128)(2,1)S(1)} collective-permute-done((bf16[160,1536]{1,0:T(8,128)(2,1)}, bf16[160,1536]{1,0:T(8,128)(2,1)S(1)}, u32[]{:S(2)}, u32[]{:S(2)}) %collective-permute-start.2) | collective-permute-done | bytes 491552 | tf_op jit(solution)/shard_map/ppermute | solution.py:220
  87.1 1.5 broadcast_in_dim.226
  88.6 3.6 %all-to-all-start.6 = ((bf16[4,8,48,640]{3,2,1,0:T(8,128)(2,1)}), bf16[4,8,48,640]{3,2,1,0:T(8,128)(2,1)S(1)}, u32[]{:S(2)}, u32[]{:S(2)}) async-start(bf16[4,8,48,640]{3,2,1,0:T(8,128)(2,1)} %broadcast_in_dim.226), calls=%async_computation.6 | async-start | bytes 3932160 | tf_op jit(solution)/shard_map/all_to_all | solution.py:373
  92.3 22.3 %all-to-all-done.6 = bf16[4,8,48,640]{3,2,1,0:T(8,128)(2,1)S(1)} async-done(((bf16[4,8,48,640]{3,2,1,0:T(8,128)(2,1)}), bf16[4,8,48,640]{3,2,1,0:T(8,128)(2,1)S(1)}, u32[]{:S(2)}, u32[]{:S(2)}) %all-to-all-start.6) | async-done | bytes 1966112 | tf_op jit(solution)/shard_map/all_to_all | solution.py:373
  114.6 1.5 copy.53
  116.4 4.8 %convert_reduce_fusion = s32[2048]{0:T(1024)S(1)} fusion(s32[2048]{0:T(1024)S(1)} %select_reduce_fusion.3, s32[2048]{0:T(1024)S(1)} %get-tuple-element.373, pred[2048]{0:T(1024)(128)(4,1)S(1)} %get-tuple-element.455), kind=kLoop, calls=%fused_computation.28 | loop fusion | flops 25163776 | bytes 26624 | tf_op jit(solution)/shard_map/reduce_sum | solution.py:321
  123.8 1.0 copy.54.slots
  125.4 15.2 %shard_map.141 = f32[1024,1536]{1,0:T(8,128)} custom-call(s32[1024,1]{1,0:T(8,128)} %copy.54.slots, bf16[1536,640]{1,0:T(8,128)(2,1)} %bitcast.19.here, bf16[1536,640]{1,0:T(8,128)(2,1)} %collective-permute-done.4.there, bf16[640,1536]{1,0:T(8,128)(2,1)} %bitcast.135, bf16[640,1536]{1,0:T(8,128)(2,1)} %collective-permute-done.5.inner_there), custom_call_target="tpu_custom_call" | custom-call | flops 8053063680 | bytes 14155776 | tf_op jit(solution)/shard_map/pallas_call | solution.py:274
  140.6 2.1 fusion.19
  143.4 3.4 %collective-permute-start.6 = (bf16[256,1536]{1,0:T(8,128)(2,1)S(1)}, bf16[256,1536]{1,0:T(8,128)(2,1)S(1)}, u32[]{:S(2)}, u32[]{:S(2)}) collective-permute-start(bf16[256,1536]{1,0:T(8,128)(2,1)S(1)} %get-tuple-element.465), channel_id=1, source_target_pairs={{0,8},{4,12},{1,9},{5,13},{2,10},{6,14},{3,11},{7,15}} | collective-permute-start | bytes 2359304 | tf_op jit(solution)/shard_map/ppermute | solution.py:225
  148.7 27.5 %collective-permute-done.6 = bf16[256,1536]{1,0:T(8,128)(2,1)S(1)} collective-permute-done((bf16[256,1536]{1,0:T(8,128)(2,1)S(1)}, bf16[256,1536]{1,0:T(8,128)(2,1)S(1)}, u32[]{:S(2)}, u32[]{:S(2)}) %collective-permute-start.6) | collective-permute-done | bytes 786464 | tf_op jit(solution)/shard_map/ppermute | solution.py:225
  176.2 3.4 %fusion.10 = (bf16[256,1536]{1,0:T(8,128)(2,1)S(1)}, bf16[256,1536]{1,0:T(8,128)(2,1)}) fusion(bf16[256,1536]{1,0:T(8,128)(2,1)S(1)} %collective-permute-done.8, f32[4,256,1536]{2,1,0:T(8,128)} %get-tuple-element.375, s32[]{:T(128)S(6)} %max.9, bf16[256,1536]{1,0:T(8,128)(2,1)S(1)} %collective-permute-done.6, s32[]{:T(128)S(6)} %select_n.292), kind=kLoop, calls=%fused_computation.45 | loop fusion | flops 2359296 | bytes 6291464 | tf_op jit(solution)/shard_map/convert_element_type | solution.py:303
  179.6 4.4 %collective-permute-start.7 = (bf16[256,1536]{1,0:T(8,128)(2,1)}, bf16[256,1536]{1,0:T(8,128)(2,1)S(1)}, u32[]{:S(2)}, u32[]{:S(2)}) collective-permute-start(bf16[256,1536]{1,0:T(8,128)(2,1)} %get-tuple-element.463), channel_id=1, source_target_pairs={{0,8},{4,12},{8,16},{12,20},{1,9},{5,13},{9,17},{13,21},{2,10},{6,... | collective-permute-start | bytes 2359304 | tf_op jit(solution)/shard_map/ppermute | solution.py:225
  185.1 1.4 convolution_convert_fusion.2
  186.5 14.7 %collective-permute-done.7 = bf16[256,1536]{1,0:T(8,128)(2,1)S(1)} collective-permute-done((bf16[256,1536]{1,0:T(8,128)(2,1)}, bf16[256,1536]{1,0:T(8,128)(2,1)S(1)}, u32[]{:S(2)}, u32[]{:S(2)}) %collective-permute-start.7) | collective-permute-done | bytes 786464 | tf_op jit(solution)/shard_map/ppermute | solution.py:225
  201.2 3.3 %fusion.12 = (bf16[256,1536]{1,0:T(8,128)(2,1)S(1)}, bf16[256,1536]{1,0:T(8,128)(2,1)}) fusion(bf16[256,1536]{1,0:T(8,128)(2,1)S(1)} %collective-permute-done.7, f32[4,256,1536]{2,1,0:T(8,128)} %get-tuple-element.375, s32[]{:T(128)S(6)} %select_n.291, bf16[256,1536]{1,0:T(8,128)(2,1)S(1)} %collective-permute-done.9, s32[]{:T(128)S(6)} %max.11), kind=kLoop, calls=%fused_computation.49 | loop fusion | flops 2359296 | bytes 6291464 | tf_op jit(solution)/shard_map/convert_element_type | solution.py:302
  204.5 1.3 collective-permute-start.14
  205.7 9.0 %collective-permute-start.13 = (bf16[256,1536]{1,0:T(8,128)(2,1)S(1)}, bf16[256,1536]{1,0:T(8,128)(2,1)S(1)}, u32[]{:S(2)}, u32[]{:S(2)}) collective-permute-start(bf16[256,1536]{1,0:T(8,128)(2,1)S(1)} %get-tuple-element.460), channel_id=1, source_target_pairs={{0,8},{4,12},{8,16},{12,20},{16,24},{20,28},{1,9},{5,13},{9,17},{1... | collective-permute-start | bytes 2359304 | tf_op jit(solution)/shard_map/ppermute | solution.py:225
  214.8 14.7 %collective-permute-done.14 = bf16[256,1536]{1,0:T(8,128)(2,1)S(1)} collective-permute-done((bf16[256,1536]{1,0:T(8,128)(2,1)}, bf16[256,1536]{1,0:T(8,128)(2,1)S(1)}, u32[]{:S(2)}, u32[]{:S(2)}) %collective-permute-start.14) | collective-permute-done | bytes 786464 | tf_op jit(solution)/shard_map/ppermute | solution.py:225
  230.5 1.7 fusion.14
  232.2 4.9 %all-to-all-start.7 = ((bf16[8,48,1280]{2,1,0:T(8,128)(2,1)}), bf16[8,48,1280]{2,1,0:T(8,128)(2,1)S(1)}, u32[]{:S(2)}, u32[]{:S(2)}) async-start(bf16[8,48,1280]{2,1,0:T(8,128)(2,1)} %bitcast.36), calls=%async_computation.7 | async-start | bytes 1966080 | tf_op jit(solution)/shard_map/all_to_all | solution.py:373
  240.0 1.2 copy.56
  241.2 12.0 %shard_map.142 = bf16[64,2,16,128]{3,2,1,0:T(8,128)(2,1)} custom-call(s32[64]{0:T(128)} %lengths.1, bf16[64,2,24,128]{3,2,1,0:T(8,128)(2,1)} %bitcast.131, bf16[64,192,256]{2,1,0:T(8,128)(2,1)} %keys.1, bf16[64,192,256]{2,1,0:T(8,128)(2,1)} %values.1), custom_call_target="tpu_custom_call" | custom-call | flops 201326592 | bytes 12582912 | tf_op jit(solution)/shard_map/pallas_call | solution.py:194
  253.2 1.2 copy.62
  254.8 7.5 %all-to-all-done.7 = bf16[8,48,1280]{2,1,0:T(8,128)(2,1)S(1)} async-done(((bf16[8,48,1280]{2,1,0:T(8,128)(2,1)}), bf16[8,48,1280]{2,1,0:T(8,128)(2,1)S(1)}, u32[]{:S(2)}, u32[]{:S(2)}) %all-to-all-start.7) | async-done | bytes 983072 | tf_op jit(solution)/shard_map/all_to_all | solution.py:373
  262.8 1.0 copy.59.heads
  263.8 7.5 %shard_map.143 = bf16[4,1280,256]{2,1,0:T(8,128)(2,1)} custom-call(bf16[5120,1024]{1,0:T(8,128)(2,1)} %all-gather.2.cloned.1.call-done.weights, bf16[1024,256]{1,0:T(8,128)(2,1)} %copy.59.heads), custom_call_target="tpu_custom_call" | custom-call | flops 2684354560 | bytes 10485760 | tf_op jit(solution)/shard_map/pallas_call | solution.py:240
  271.4 4.5 %all-to-all-start.8 = ((bf16[4,1280,256]{2,1,0:T(8,128)(2,1)}), bf16[4,1280,256]{2,1,0:T(8,128)(2,1)}, u32[]{:S(2)}, u32[]{:S(2)}) async-start(bf16[4,1280,256]{2,1,0:T(8,128)(2,1)} %shard_map.143), calls=%async_computation.8 | async-start | bytes 5242880 | tf_op jit(solution)/shard_map/all_to_all | solution.py:373
  276.2 30.4 %all-to-all-done.8 = bf16[4,1280,256]{2,1,0:T(8,128)(2,1)} async-done(((bf16[4,1280,256]{2,1,0:T(8,128)(2,1)}), bf16[4,1280,256]{2,1,0:T(8,128)(2,1)}, u32[]{:S(2)}, u32[]{:S(2)}) %all-to-all-start.8) | async-done | bytes 2621472 | tf_op jit(solution)/shard_map/all_to_all | solution.py:373
  306.6 2.2 convert_reduce_fusion.2
  309.0 1.5 collective-permute-start.17
  310.5 1.5 collective-permute-start.16
  314.1 1.5 collective-permute-done.15
  (84 shorter events, 20.0 us)
Async XLA Ops:
  11.7 11.4 %copy-start.7 = (f32[5120]{0:T(1024)S(1)}, f32[5120]{0:T(1024)}, u32[]{:S(2)}) copy-start(f32[5120]{0:T(1024)} %param.20) | copy-start | bytes 61444
  17.9 14.4 %all-to-all-start.4 = ((bf16[4,48,1280]{2,1,0:T(8,128)(2,1)}), bf16[4,48,1280]{2,1,0:T(8,128)(2,1)S(1)}, u32[]{:S(2)}, u32[]{:S(2)}) async-start(bf16[4,48,1280]{2,1,0:T(8,128)(2,1)} %bitcast.128), calls=%async_computation.4 | async-start | bytes 983040 | tf_op jit(solution)/shard_map/all_to_all | solution.py:373
  32.5 6.8 %copy-start.2 = (bf16[4,160,1024]{2,1,0:T(8,128)(2,1)S(1)}, bf16[4,160,1024]{2,1,0:T(8,128)(2,1)}, u32[]{:S(2)}) copy-start(bf16[4,160,1024]{2,1,0:T(8,128)(2,1)} %get-tuple-element.376) | copy-start | bytes 3932164
  33.6 21.8 %all-to-all-start.5 = ((bf16[8,48,640]{2,1,0:T(8,128)(2,1)}), bf16[8,48,640]{2,1,0:T(8,128)(2,1)S(1)}, u32[]{:S(2)}, u32[]{:S(2)}) async-start(bf16[8,48,640]{2,1,0:T(8,128)(2,1)} %bitcast.9), calls=%async_computation.5 | async-start | bytes 983040 | tf_op jit(solution)/shard_map/all_to_all | solution.py:373
  39.2 162.0 %all-gather.2.cloned.1.call-start = ((), (), s32[]{:S(2)}) async-start(), calls=%async_computation.9 | async-start | bytes 11796480 | tf_op jit(solution)/shard_map/all_gather | solution.py:394
  40.1 20.1 %collective-permute-start.10 = (bf16[160,1024]{1,0:T(8,128)(2,1)S(1)}, bf16[160,1024]{1,0:T(8,128)(2,1)}, u32[]{:S(2)}, u32[]{:S(2)}) collective-permute-start(bf16[160,1024]{1,0:T(8,128)(2,1)S(1)} %get-tuple-element.472), channel_id=1, source_target_pairs={{0,1},{1,0},{2,3},{3,2},{4,5},{5,4},{6,7},{7,6},{8,9},{9,8},{10,11... | collective-permute-start | bytes 983048 | tf_op jit(solution)/shard_map/ppermute | solution.py:220
  42.1 19.1 %collective-permute-start.11 = (bf16[160,1024]{1,0:T(8,128)(2,1)S(1)}, bf16[160,1024]{1,0:T(8,128)(2,1)}, u32[]{:S(2)}, u32[]{:S(2)}) collective-permute-start(bf16[160,1024]{1,0:T(8,128)(2,1)S(1)} %get-tuple-element.471), channel_id=1, source_target_pairs={{0,2},{1,3},{2,0},{3,1},{4,6},{5,7},{6,4},{7,5},{8,10},{9,11},{10,... | collective-permute-start | bytes 983048 | tf_op jit(solution)/shard_map/ppermute | solution.py:220
  43.6 20.1 %collective-permute-start.12 = (bf16[160,1024]{1,0:T(8,128)(2,1)}, bf16[160,1024]{1,0:T(8,128)(2,1)}, u32[]{:S(2)}, u32[]{:S(2)}) collective-permute-start(bf16[160,1024]{1,0:T(8,128)(2,1)} %get-tuple-element.470), channel_id=1, source_target_pairs={{0,3},{1,2},{2,1},{3,0},{4,7},{5,6},{6,5},{7,4},{8,11},{9,10},{10,... | collective-permute-start | bytes 983048 | tf_op jit(solution)/shard_map/ppermute | solution.py:220
  58.2 14.3 %collective-permute-start.1 = (bf16[160,1536]{1,0:T(8,128)(2,1)}, bf16[160,1536]{1,0:T(8,128)(2,1)S(1)}, u32[]{:S(2)}, u32[]{:S(2)}) collective-permute-start(bf16[160,1536]{1,0:T(8,128)(2,1)} %get-tuple-element.468), channel_id=1, source_target_pairs={{0,1},{1,0},{2,3},{3,2},{4,5},{5,4},{6,7},{7,6},{8,9},{9,8},{10,11... | collective-permute-start | bytes 1474568 | tf_op jit(solution)/shard_map/ppermute | solution.py:220
  62.2 23.3 %collective-permute-start.2 = (bf16[160,1536]{1,0:T(8,128)(2,1)}, bf16[160,1536]{1,0:T(8,128)(2,1)S(1)}, u32[]{:S(2)}, u32[]{:S(2)}) collective-permute-start(bf16[160,1536]{1,0:T(8,128)(2,1)} %get-tuple-element.467), channel_id=1, source_target_pairs={{0,2},{1,3},{2,0},{3,1},{4,6},{5,7},{6,4},{7,5},{8,10},{9,11},{10,... | collective-permute-start | bytes 1474568 | tf_op jit(solution)/shard_map/ppermute | solution.py:220
  64.7 1.1 copy-start.3
  65.8 20.5 %collective-permute-start.3 = (bf16[160,1536]{1,0:T(8,128)(2,1)}, bf16[160,1536]{1,0:T(8,128)(2,1)S(1)}, u32[]{:S(2)}, u32[]{:S(2)}) collective-permute-start(bf16[160,1536]{1,0:T(8,128)(2,1)} %get-tuple-element.466), channel_id=1, source_target_pairs={{0,3},{1,2},{2,1},{3,0},{4,7},{5,6},{6,5},{7,4},{8,11},{9,10},{10,... | collective-permute-start | bytes 1474568 | tf_op jit(solution)/shard_map/ppermute | solution.py:220
  88.6 26.0 %all-to-all-start.6 = ((bf16[4,8,48,640]{3,2,1,0:T(8,128)(2,1)}), bf16[4,8,48,640]{3,2,1,0:T(8,128)(2,1)S(1)}, u32[]{:S(2)}, u32[]{:S(2)}) async-start(bf16[4,8,48,640]{3,2,1,0:T(8,128)(2,1)} %broadcast_in_dim.226), calls=%async_computation.6 | async-start | bytes 3932160 | tf_op jit(solution)/shard_map/all_to_all | solution.py:373
  92.2 33.2 %collective-permute-start.5 = (bf16[640,1536]{1,0:T(8,128)(2,1)}, bf16[640,1536]{1,0:T(8,128)(2,1)}, u32[]{:S(2)}, u32[]{:S(2)}) collective-permute-start(bf16[640,1536]{1,0:T(8,128)(2,1)} %bitcast.134), channel_id=1, source_target_pairs={{0,4},{4,0},{8,12},{12,8},{16,20},{20,16},{24,28},{28,24},{1,5},{5... | collective-permute-start | bytes 5898248 | tf_op jit(solution)/shard_map/ppermute | solution.py:220
  116.1 9.3 %collective-permute-start.4 = (bf16[1536,640]{1,0:T(8,128)(2,1)}, bf16[1536,640]{1,0:T(8,128)(2,1)}, u32[]{:S(2)}, u32[]{:S(2)}) collective-permute-start(bf16[1536,640]{1,0:T(8,128)(2,1)} %bitcast.19.here), channel_id=1, source_target_pairs={{0,4},{4,0},{8,12},{12,8},{16,20},{20,16},{24,28},{28,24},{1,5},{5... | collective-permute-start | bytes 5898248 | tf_op jit(solution)/shard_map/ppermute | solution.py:220
  121.2 19.5 %copy-start.5 = (s32[2048]{0:T(1024)}, s32[2048]{0:T(1024)S(1)}, u32[]{:S(2)}) copy-start(s32[2048]{0:T(1024)S(1)} %convert_reduce_fusion) | copy-start | bytes 24580
  142.7 6.0 %collective-permute-start.8 = (bf16[256,1536]{1,0:T(8,128)(2,1)S(1)}, bf16[256,1536]{1,0:T(8,128)(2,1)S(1)}, u32[]{:S(2)}, u32[]{:S(2)}) collective-permute-start(bf16[256,1536]{1,0:T(8,128)(2,1)S(1)} %get-tuple-element.464), channel_id=1, source_target_pairs={{24,16},{28,20},{25,17},{29,21},{26,18},{30,22},{27,19},{31,23}} | collective-permute-start | bytes 2359304 | tf_op jit(solution)/shard_map/ppermute | solution.py:225
  143.4 32.8 %collective-permute-start.6 = (bf16[256,1536]{1,0:T(8,128)(2,1)S(1)}, bf16[256,1536]{1,0:T(8,128)(2,1)S(1)}, u32[]{:S(2)}, u32[]{:S(2)}) collective-permute-start(bf16[256,1536]{1,0:T(8,128)(2,1)S(1)} %get-tuple-element.465), channel_id=1, source_target_pairs={{0,8},{4,12},{1,9},{5,13},{2,10},{6,14},{3,11},{7,15}} | collective-permute-start | bytes 2359304 | tf_op jit(solution)/shard_map/ppermute | solution.py:225
  148.7 36.0 %copy-start.8 = (s32[8,256]{1,0:T(8,128)S(1)}, s32[8,256]{1,0:T(8,128)}, u32[]{:S(2)}) copy-start(s32[8,256]{1,0:T(8,128)} %add.302) | copy-start | bytes 24580
  148.7 36.4 %copy-start.4 = (bf16[192,1280]{1,0:T(8,128)(2,1)S(1)}, bf16[192,1280]{1,0:T(8,128)(2,1)}, u32[]{:S(2)}) copy-start(bf16[192,1280]{1,0:T(8,128)(2,1)} %shard_map.138) | copy-start | bytes 1474564
  179.6 21.6 %collective-permute-start.7 = (bf16[256,1536]{1,0:T(8,128)(2,1)}, bf16[256,1536]{1,0:T(8,128)(2,1)S(1)}, u32[]{:S(2)}, u32[]{:S(2)}) collective-permute-start(bf16[256,1536]{1,0:T(8,128)(2,1)} %get-tuple-element.463), channel_id=1, source_target_pairs={{0,8},{4,12},{8,16},{12,20},{1,9},{5,13},{9,17},{13,21},{2,10},{6,... | collective-permute-start | bytes 2359304 | tf_op jit(solution)/shard_map/ppermute | solution.py:225
  184.0 17.2 %collective-permute-start.9 = (bf16[256,1536]{1,0:T(8,128)(2,1)S(1)}, bf16[256,1536]{1,0:T(8,128)(2,1)S(1)}, u32[]{:S(2)}, u32[]{:S(2)}) collective-permute-start(bf16[256,1536]{1,0:T(8,128)(2,1)S(1)} %get-tuple-element.462), channel_id=1, source_target_pairs={{16,8},{20,12},{24,16},{28,20},{17,9},{21,13},{25,17},{29,21},{18,... | collective-permute-start | bytes 2359304 | tf_op jit(solution)/shard_map/ppermute | solution.py:225
  204.5 25.0 %collective-permute-start.14 = (bf16[256,1536]{1,0:T(8,128)(2,1)}, bf16[256,1536]{1,0:T(8,128)(2,1)S(1)}, u32[]{:S(2)}, u32[]{:S(2)}) collective-permute-start(bf16[256,1536]{1,0:T(8,128)(2,1)} %get-tuple-element.461), channel_id=1, source_target_pairs={{8,0},{12,4},{16,8},{20,12},{24,16},{28,20},{9,1},{13,5},{17,9},{2... | collective-permute-start | bytes 2359304 | tf_op jit(solution)/shard_map/ppermute | solution.py:225
  205.7 24.7 %collective-permute-start.13 = (bf16[256,1536]{1,0:T(8,128)(2,1)S(1)}, bf16[256,1536]{1,0:T(8,128)(2,1)S(1)}, u32[]{:S(2)}, u32[]{:S(2)}) collective-permute-start(bf16[256,1536]{1,0:T(8,128)(2,1)S(1)} %get-tuple-element.460), channel_id=1, source_target_pairs={{0,8},{4,12},{8,16},{12,20},{16,24},{20,28},{1,9},{5,13},{9,17},{1... | collective-permute-start | bytes 2359304 | tf_op jit(solution)/shard_map/ppermute | solution.py:225
  232.2 30.1 %all-to-all-start.7 = ((bf16[8,48,1280]{2,1,0:T(8,128)(2,1)}), bf16[8,48,1280]{2,1,0:T(8,128)(2,1)S(1)}, u32[]{:S(2)}, u32[]{:S(2)}) async-start(bf16[8,48,1280]{2,1,0:T(8,128)(2,1)} %bitcast.36), calls=%async_computation.7 | async-start | bytes 1966080 | tf_op jit(solution)/shard_map/all_to_all | solution.py:373
  263.8 7.5 %copy-start.6 = (s32[2048]{0:T(1024)S(1)}, s32[2048]{0:T(1024)}, u32[]{:S(2)}) copy-start(s32[2048]{0:T(1024)} %copy-done.5) | copy-start | bytes 24580
  271.4 35.2 %all-to-all-start.8 = ((bf16[4,1280,256]{2,1,0:T(8,128)(2,1)}), bf16[4,1280,256]{2,1,0:T(8,128)(2,1)}, u32[]{:S(2)}, u32[]{:S(2)}) async-start(bf16[4,1280,256]{2,1,0:T(8,128)(2,1)} %shard_map.143), calls=%async_computation.8 | async-start | bytes 5242880 | tf_op jit(solution)/shard_map/all_to_all | solution.py:373
  309.0 4.5 %collective-permute-start.17 = (f32[256]{0:T(256)S(1)}, f32[256]{0:T(256)S(1)}, u32[]{:S(2)}, u32[]{:S(2)}) collective-permute-start(f32[256]{0:T(256)S(1)} %multiply_reduce_fusion), channel_id=1, source_target_pairs={{0,3},{1,2},{2,1},{3,0},{4,7},{5,6},{6,5},{7,4},{8,11},{9,10},{10,... | collective-permute-start | bytes 3080 | tf_op jit(solution)/shard_map/ppermute | solution.py:220
  310.5 3.6 %collective-permute-start.16 = (f32[256]{0:T(256)S(1)}, f32[256]{0:T(256)S(1)}, u32[]{:S(2)}, u32[]{:S(2)}) collective-permute-start(f32[256]{0:T(256)S(1)} %multiply_reduce_fusion), channel_id=1, source_target_pairs={{0,2},{1,3},{2,0},{3,1},{4,6},{5,7},{6,4},{7,5},{8,10},{9,11},{10,... | collective-permute-start | bytes 3080 | tf_op jit(solution)/shard_map/ppermute | solution.py:220
  312.0 3.6 %collective-permute-start.15 = (f32[256]{0:T(256)S(1)}, f32[256]{0:T(256)S(1)}, u32[]{:S(2)}, u32[]{:S(2)}) collective-permute-start(f32[256]{0:T(256)S(1)} %multiply_reduce_fusion), channel_id=1, source_target_pairs={{0,1},{1,0},{2,3},{3,2},{4,5},{5,4},{6,7},{7,6},{8,9},{9,8},{10,11... | collective-permute-start | bytes 3080 | tf_op jit(solution)/shard_map/ppermute | solution.py:220
Sparse Core Ops, SparseCore 0:
  65.9 105.5 all-gather.1

commit v2 on v1

--- a/solution.py
+++ b/solution.py
@@ -17,7 +17,8 @@
 SLOTS = 192
 ROW_SLOTS = 48
 PROJECT_STEPS = 2
-ATTEND_ROWS = 8
+ATTEND_ROWS = 16
+SUM_PARTS = 2
 
 
 beta_one = 0.9
@@ -169,8 +170,9 @@
         cached = jnp.exp(cached - top)
         new = jnp.exp(new - top)
         total = jnp.sum(cached, axis=-1, keepdims=True) + jnp.sum(new, axis=-1, keepdims=True)
+        share = 1.0 / total
         probs.append(
-            ((cached / total).astype(jnp.bfloat16), (new / total).astype(jnp.bfloat16), both)
+            ((cached * share).astype(jnp.bfloat16), (new * share).astype(jnp.bfloat16), both)
         )
     for row in range(rows):
         for group in range(groups):
@@ -234,22 +236,22 @@
     out[0] = found.astype(out.dtype)
 
 
-def outward(weights, heads, n_tp):
+def outward(weights, heads, blocks):
     depth, count = heads.shape
-    width = weights.shape[0] // n_tp
+    width = weights.shape[0] // blocks
     return pl.pallas_call(
         outward_body,
-        grid=(n_tp,),
+        grid=(blocks,),
         in_specs=[
             pl.BlockSpec((width, depth), lambda i: (i, 0)),
             pl.BlockSpec((depth, count), lambda i: (0, 0)),
         ],
         out_specs=pl.BlockSpec((1, width, count), lambda i: (i, 0, 0)),
-        out_shape=jax.ShapeDtypeStruct((n_tp, width, count), jnp.bfloat16),
+        out_shape=jax.ShapeDtypeStruct((blocks, width, count), jnp.bfloat16),
         compiler_params=pltpu.CompilerParams(vmem_limit_bytes=56 * 2**20),
         cost_estimate=pl.CostEstimate(
-            flops=2 * count * depth * width * n_tp,
-            bytes_accessed=2 * depth * width * n_tp,
+            flops=2 * count * depth * width * blocks,
+            bytes_accessed=2 * depth * width * blocks,
             transcendentals=0,
         ),
     )(weights, heads)
@@ -292,18 +294,27 @@
     return lax.optimization_barrier((values, others))
 
 
-def line_sum(block, plane, planes, late):
-    right = left = None
+def line_sum(terms, plane, planes, late):
+    width = terms.shape[2] // SUM_PARTS
+    block = lambda d, part: lax.dynamic_slice(
+        terms, (d, 0, part * width), (1, terms.shape[1], width)
+    )[0]
+    right, left = [None] * SUM_PARTS, [None] * SUM_PARTS
     for step in range(1, planes):
-        forth = block(jnp.minimum(plane + planes - step, planes - 1))
-        back = block(jnp.maximum(plane - planes + step, 0))
-        if right is not None:
-            forth, back = forth + right, back + left
-        right = hop(forth.astype(jnp.bfloat16), 0, step, 1)
-        left = hop(back.astype(jnp.bfloat16), planes - step, planes, -1)
+        for part in range(SUM_PARTS):
+            forth = block(jnp.minimum(plane + planes - step, planes - 1), part)
+            back = block(jnp.maximum(plane - planes + step, 0), part)
+            if step > 1:
+                forth, back = forth + right[part], back + left[part]
+            right[part] = hop(forth.astype(jnp.bfloat16), 0, step, 1)
+            left[part] = hop(back.astype(jnp.bfloat16), planes - step, planes, -1)
         if step == max(planes - 2, 1):
             (right, left), (late,) = tie((right, left), late)
-    return block(plane) + right.astype(jnp.float32) + left.astype(jnp.float32), late
+    sums = [
+        block(plane, part) + right[part].astype(jnp.float32) + left[part].astype(jnp.float32)
+        for part in range(SUM_PARTS)
+    ]
+    return jnp.concatenate(sums, axis=1), late
 
 
 def leaders(ids):
@@ -344,8 +355,9 @@
     out = lax.dynamic_update_index_in_dim(blocks, block_of(blocks, place), place, 0)
     for mask in range(1, n):
         got = flip(block_of(blocks, place ^ mask), axis, mask)
+        early = got if mask == 1 else early
         out = lax.dynamic_update_index_in_dim(out, got, place ^ mask, 0)
-    return out
+    return out, early
 
 
 def shards(
@@ -390,7 +402,7 @@
     weights_in, _ = tie(weights_in, rows)
     *partial, outer = adam(weights_in, (), n_tp, INNER, OUTER)
     swapped, (outer,) = tie(swapped, outer)
-    outer = exchange(outer, "tp", tp).reshape(depth, -1)
+    outer = exchange(outer, "tp", tp)[0].reshape(depth, -1)
     out_weights = lax.all_gather(outer, "rep", axis=0, tiled=True)
 
     def normed_rows(found):
@@ -403,16 +415,23 @@
         return normed_in.reshape(n_rep, share, depth)
 
     def all_slots(got):
-        got = swap(jnp.broadcast_to(got[None], (n_tp,) + got.shape))
-        return got.transpose(1, 0, 2, 3).reshape(-1, depth)
+        got = got.reshape(-1, depth)
+        return jnp.concatenate([got] + [flip(got, "tp", mask) for mask in range(1, n_tp)])
+
+    def slot_from(block, number, low):
+        slot = number - low
+        share = SLOTS // n_tp
+        at = ((slot // share) ^ tp) * n_rep * share + block * share + slot % share
+        return jnp.where((slot >= 0) & (slot < SLOTS), at, -1)
 
     normed_in = normed_rows(swapped)
     got = swap(normed_in, "rep")
     (weights_in, partial), _ = tie((weights_in, partial), normed_in)
     updated, new_first, second, inner = adam(weights_in, partial, n_tp, 0, INNER)
     got, (inner,) = tie(got, inner)
-    inner = exchange(inner, "tp", tp).reshape(depth, -1)
-    got, (inner,) = tie(got, inner)
+    inner, first_flip = exchange(inner, "tp", tp)
+    got, _ = tie(got, first_flip)
+    inner = inner.reshape(depth, -1)
     inner_other = flip(inner, "rep", 1)
 
     here = all_slots(got)
@@ -423,16 +442,17 @@
     ).reshape(-1)
     core_block, core_number = core_tokens(flat_block), core_tokens(number)
     rounds = jnp.max(number) // SLOTS + 1
-
-    def terms_of(here, turn):
-        slot = slot_of(core_block, core_number, turn * SLOTS, SLOTS)
-        return project(slot[:, None], here, flip(here, "rep", 1), inner, inner_other, planes)
+    slot_at = lambda turn: slot_from(core_block, core_number, turn * SLOTS)[:, None]
+    here, (first_slots, rounds) = tie(here, slot_at(0), rounds)
+
+    def terms_of(here, slots):
+        return project(slots, here, flip(here, "rep", 1), inner, inner_other, planes)
 
     def terms_again(turn):
         found = swap(fetch(turn).reshape(n_tp, -1, width_local))
-        return terms_of(all_slots(swap(normed_rows(found), "rep")), turn)
-
-    terms = terms_of(here, 0)
+        return terms_of(all_slots(swap(normed_rows(found), "rep")), slot_at(turn))
+
+    terms = terms_of(here, first_slots)
     terms = lax.fori_loop(1, rounds, lambda turn, kept: kept + terms_again(turn), terms)
 
     ids, _ = tie(ids, terms)
@@ -448,19 +468,18 @@
         return picked(slot, found).reshape(n_rep, ROW_SLOTS, width_local)
 
     def own_rows(far, sent):
-        found = swap(sent, "rep").reshape(-1, width_local)
+        found = exchange(sent, "rep", rep)[0].reshape(-1, width_local)
         return picked(slot_of(my_block, my_number, far * ROW_SLOTS, ROW_SLOTS), found)
 
     sent = to_send(0, 0, rows)
-    projected, (out_weights, sent) = line_sum(
-        lambda d: block_of(terms, d), plane, planes, (out_weights, sent)
-    )
+    projected, (out_weights, sent) = line_sum(terms, plane, planes, (out_weights, sent))
     projected = projected.astype(jnp.bfloat16)
-    sent, _ = tie(sent, projected)
+    heads = attend(projected, cache_keys, stored_values, lengths)
+    partial_out = outward(out_weights, heads, 2).reshape(n_tp, width_local, count)
+    attended = swap(partial_out)
+    sent, _ = tie(sent, partial_out)
     own_cols = own_rows(0, sent)
-
-    heads = attend(projected, cache_keys, stored_values, lengths)
-    heads, (own_cols,) = tie(heads, own_cols)
+    attended, (own_cols,) = tie(attended, own_cols)
     own_cols = lax.fori_loop(
         1,
         (jnp.max(row_number) // ROW_SLOTS + 1) * rounds,
@@ -470,9 +489,7 @@
         ),
         own_cols,
     )
-
-    partial_out = outward(out_weights, heads, n_tp)
-    attended = jnp.sum(swap(partial_out).astype(jnp.float32), axis=0).T
+    attended = jnp.sum(attended.astype(jnp.float32), axis=0).T
     resid = own_cols.astype(jnp.float32) + attended
     square = jnp.sum(resid * resid, axis=-1)
     total = functools.reduce(

time: 325 us -> 308 us (0.948)
  waiting for transfers between devices: 139 us -> 104 us
  starting transfers between devices: 54.2 us -> 71.5 us
  other arithmetic: 23.3 us -> 28.2 us
    all_to_all x5 -> x3, waiting for transfers between devices: 60.2 us -> 8.43 us  [shards(): lax.all_to_all(values, axis, split_axis=0, concat_axis=0, tiled=True)]
    ppermute x11 -> x21, waiting for transfers between devices: 20.9 us -> 42.4 us  [flip(): return lax.ppermute(values, axis, [(i, i ^ bit) for i in range(n)])]
    ppermute x11 -> x21, starting transfers between devices: 10.7 us -> 24.1 us  [flip(): return lax.ppermute(values, axis, [(i, i ^ bit) for i in range(n)])]
    ppermute x6 -> x12, starting transfers between devices: 19.5 us -> 31.8 us  [hop(): return lax.ppermute(values, 'rep', pairs)]
    all_to_all x5 -> x3, starting transfers between devices: 23.9 us -> 15.3 us  [shards(): lax.all_to_all(values, axis, split_axis=0, concat_axis=0, tiled=True)]
    convert_element_type x3 -> x2, other arithmetic: 8.34 us -> 3.71 us  [the longest x1 2.18 us: line_sum(): left[part] = hop(back.astype(jnp.bfloat16), planes - step, planes, -1)]
    ppermute x6 -> x12, waiting for transfers between devices: 57.9 us -> 53.4 us  [hop(): return lax.ppermute(values, 'rep', pairs)]
  transfers between devices with their start and end apart: 23 -> 37, of which waited for: 12 -> 18; matrix products, arithmetic and copies ran while one was open for 10% -> 10% of each run, Pallas kernels for 15% -> 12%
where the time goes in v2:
time: 308 us; the launch traced here: 306 us
  waiting for transfers between devices  104 us (34%)
  starting transfers between devices  71.5 us (23%)
  Pallas kernels  59.4 us (19%)
  other arithmetic  28.2 us (9%)
  local copies, waits for them, and re-layouts  23.2 us (8%)
  between operations  18.7 us (6%)
    ppermute x12, waiting for transfers between devices, hop(): return lax.ppermute(values, 'rep', pairs)  53.4 us
    ppermute x21, waiting for transfers between devices, flip(): return lax.ppermute(values, axis, [(i, i ^ bit) for i in range(n)])  42.4 us
    ppermute x12, starting transfers between devices, hop(): return lax.ppermute(values, 'rep', pairs)  31.8 us
    ppermute x21, starting transfers between devices, flip(): return lax.ppermute(values, axis, [(i, i ^ bit) for i in range(n)])  24.1 us
    pallas_call x2, Pallas kernels, adam(): pl.pallas_call(adam_body, grid=(groups,), in_specs=[part] * 4 + [pl.Block...  21 us
    all_to_all x3, starting transfers between devices, shards(): lax.all_to_all(values, axis, split_axis=0, concat_axis=0, tiled=True)  15.3 us
    pallas_call x1, Pallas kernels, project(): pl.pallas_call(project_body, grid=(PROJECT_STEPS,), in_specs=[pl.BlockSpe...  15.3 us
    pallas_call x1, Pallas kernels, attend(): pl.pallas_call(attend_body, grid_spec=pltpu.PrefetchScalarGridSpec(num_sc...  10.4 us
  transfers between devices with their start and end apart: 37, of which 18 were waited for; matrix products, arithmetic and copies ran while one was open for 10% of the time, Pallas kernels for 12%

profile of v2, /device:TPU:0, one launch (start us, length us, event | category | flops | bytes accessed | tf_op | source)
XLA Modules:
  0.0 306.3 jit_solution(16457368362868514727)
XLA Ops:
  8.2 2.3 select_reduce_fusion.3
  12.3 5.9 %shard_map.138 = bf16[192,1280]{1,0:T(8,128)(2,1)} custom-call(s32[192]{0:T(256)} %select_reduce_fusion.5.ids, bf16[9600,1280]{1,0:T(8,128)(2,1)} %embed.1), custom_call_target="tpu_custom_call" | custom-call | bytes 9830400 | tf_op jit(solution)/shard_map/pallas_call | solution.py:118
  18.2 5.2 %all-to-all-start.2 = ((bf16[4,48,1280]{2,1,0:T(8,128)(2,1)}), bf16[4,48,1280]{2,1,0:T(8,128)(2,1)S(1)}, u32[]{:S(2)}, u32[]{:S(2)}) async-start(bf16[4,48,1280]{2,1,0:T(8,128)(2,1)} %bitcast.238), calls=%async_computation.2 | async-start | bytes 983040 | tf_op jit(solution)/shard_map/all_to_all | solution.py:385
  23.4 9.2 %shard_map.139 = (f32[160,10240]{1,0:T(8,128)}, f32[160,10240]{1,0:T(8,128)}, f32[160,10240]{1,0:T(8,128)}, bf16[4,160,1024]{2,1,0:T(8,128)(2,1)}) custom-call(f32[160,10240]{1,0:T(8,128)} %master.1, f32[160,10240]{1,0:T(8,128)} %moment.1, f32[160,10240]{1,0:T(8,128)} %variance.1, bf16[160,10240]{1,0:T(8,128)(2,1)} %grads.1), custom_call_target="tpu_custom_call" | custom-call | flops 9830400 | bytes 18350080 | tf_op jit(solution)/shard_map/pallas_call | solution.py:56
  33.9 5.6 %all-to-all-start.3 = ((bf16[8,48,640]{2,1,0:T(8,128)(2,1)}), bf16[8,48,640]{2,1,0:T(8,128)(2,1)S(1)}, u32[]{:S(2)}, u32[]{:S(2)}) async-start(bf16[8,48,640]{2,1,0:T(8,128)(2,1)} %bitcast.24), calls=%async_computation.3 | async-start | bytes 983040 | tf_op jit(solution)/shard_map/all_to_all | solution.py:385
  40.7 2.0 collective-permute-start.27
  42.7 1.5 collective-permute-start.28
  44.2 11.8 %shard_map.140 = (f32[160,10240]{1,0:T(8,128)}, f32[160,10240]{1,0:T(8,128)}, f32[160,10240]{1,0:T(8,128)}, bf16[4,160,1536]{2,1,0:T(8,128)(2,1)}) custom-call(f32[160,10240]{1,0:T(8,128)} %master.1, f32[160,10240]{1,0:T(8,128)} %moment.1, f32[160,10240]{1,0:T(8,128)} %variance.1, ...), custom_call_target="tpu_custom_call", output_to_operand_aliasing={{0}: (4, {}), {1}: (5, {}), {2}: (6, {})} | custom-call | flops 14745600 | bytes 27525120 | tf_op jit(solution)/shard_map/pallas_call | solution.py:56
  56.0 2.7 dynamic-slice_bitcast_fusion.7
  58.7 2.0 collective-permute-start.11
  64.7 1.6 collective-permute-start.16
  66.3 6.4 %collective-permute-done.11 = bf16[160,1536]{1,0:T(8,128)(2,1)S(1)} collective-permute-done((bf16[160,1536]{1,0:T(8,128)(2,1)S(1)}, bf16[160,1536]{1,0:T(8,128)(2,1)S(1)}, u32[]{:S(2)}, u32[]{:S(2)}) %collective-permute-start.11) | collective-permute-done | bytes 491552 | tf_op jit(solution)/shard_map/ppermute | solution.py:222
  72.8 2.9 collective-permute-start.14
  76.9 5.2 %convert_reduce_fusion = s32[2048]{0:T(1024)S(1)} fusion(s32[2048]{0:T(1024)} %copy-done.21, s32[2048]{0:T(1024)} %get-tuple-element.605, pred[2048]{0:T(1024)(128)(4,1)} %get-tuple-element.710), kind=kLoop, calls=%fused_computation.56 | loop fusion | flops 25163776 | bytes 26624 | tf_op jit(solution)/shard_map/reduce_sum | solution.py:332
  86.9 13.3 %collective-permute-done.16 = bf16[160,1536]{1,0:T(8,128)(2,1)S(1)} collective-permute-done((bf16[160,1536]{1,0:T(8,128)(2,1)}, bf16[160,1536]{1,0:T(8,128)(2,1)S(1)}, u32[]{:S(2)}, u32[]{:S(2)}) %collective-permute-start.16) | collective-permute-done | bytes 491552 | tf_op jit(solution)/shard_map/ppermute | solution.py:222
  103.9 5.1 %collective-permute-done.13 = bf16[384,640]{1,0:T(8,128)(2,1)} collective-permute-done((bf16[384,640]{1,0:T(8,128)(2,1)S(1)}, bf16[384,640]{1,0:T(8,128)(2,1)}, u32[]{:S(2)}, u32[]{:S(2)}) %collective-permute-start.13) | collective-permute-done | bytes 491552 | tf_op jit(solution)/shard_map/ppermute | solution.py:222
  109.0 2.8 pad_maximum_fusion.2.here
  113.3 2.9 collective-permute-done.15.there
  116.1 15.3 %shard_map.141 = f32[1024,1536]{1,0:T(8,128)} custom-call(s32[1024,1]{1,0:T(8,128)} %fusion.33.slots, bf16[1536,640]{1,0:T(8,128)(2,1)} %pad_maximum_fusion.2.here, bf16[1536,640]{1,0:T(8,128)(2,1)} %collective-permute-done.15.there, bf16[640,1536]{1,0:T(8,128)(2,1)} %bitcast.244, bf16[640,1536]{1,0:T(8,128)(2,1)} %collective-permute-done.18.inner_there), custom_call_target="tpu_custom_call" | custom-call | flops 8053063680 | bytes 14155776 | tf_op jit(solution)/shard_map/pallas_call | solution.py:276
  131.4 2.0 fusion.37
  134.8 3.8 %collective-permute-start.21 = (bf16[256,768]{1,0:T(8,128)(2,1)S(1)}, bf16[256,768]{1,0:T(8,128)(2,1)S(1)}, u32[]{:S(2)}, u32[]{:S(2)}) collective-permute-start(bf16[256,768]{1,0:T(8,128)(2,1)S(1)} %get-tuple-element.739), channel_id=1, source_target_pairs={{0,8},{4,12},{1,9},{5,13},{2,10},{6,14},{3,11},{7,15}} | collective-permute-start | bytes 1179656 | tf_op jit(solution)/shard_map/ppermute | solution.py:227
  138.6 1.3 collective-permute-start.19
  142.2 14.3 %collective-permute-done.21 = bf16[256,768]{1,0:T(8,128)(2,1)S(1)} collective-permute-done((bf16[256,768]{1,0:T(8,128)(2,1)S(1)}, bf16[256,768]{1,0:T(8,128)(2,1)S(1)}, u32[]{:S(2)}, u32[]{:S(2)}) %collective-permute-start.21) | collective-permute-done | bytes 393248 | tf_op jit(solution)/shard_map/ppermute | solution.py:227
  156.5 16.6 %collective-permute-done.19 = bf16[256,768]{1,0:T(8,128)(2,1)S(1)} collective-permute-done((bf16[256,768]{1,0:T(8,128)(2,1)S(1)}, bf16[256,768]{1,0:T(8,128)(2,1)S(1)}, u32[]{:S(2)}, u32[]{:S(2)}) %collective-permute-start.19) | collective-permute-done | bytes 393248 | tf_op jit(solution)/shard_map/ppermute | solution.py:227
  173.1 2.2 fusion.25
  175.3 4.4 %collective-permute-start.20 = (bf16[256,768]{1,0:T(8,128)(2,1)S(1)}, bf16[256,768]{1,0:T(8,128)(2,1)S(1)}, u32[]{:S(2)}, u32[]{:S(2)}) collective-permute-start(bf16[256,768]{1,0:T(8,128)(2,1)S(1)} %get-tuple-element.736), channel_id=1, source_target_pairs={{0,8},{4,12},{8,16},{12,20},{1,9},{5,13},{9,17},{13,21},{2,10},{6,... | collective-permute-start | bytes 1179656 | tf_op jit(solution)/shard_map/ppermute | solution.py:227
  179.7 1.9 collective-permute-start.22
  183.5 5.7 %collective-permute-done.20 = bf16[256,768]{1,0:T(8,128)(2,1)S(1)} collective-permute-done((bf16[256,768]{1,0:T(8,128)(2,1)S(1)}, bf16[256,768]{1,0:T(8,128)(2,1)S(1)}, u32[]{:S(2)}, u32[]{:S(2)}) %collective-permute-start.20) | collective-permute-done | bytes 393248 | tf_op jit(solution)/shard_map/ppermute | solution.py:227
  189.2 6.8 %collective-permute-done.22 = bf16[256,768]{1,0:T(8,128)(2,1)S(1)} collective-permute-done((bf16[256,768]{1,0:T(8,128)(2,1)S(1)}, bf16[256,768]{1,0:T(8,128)(2,1)S(1)}, u32[]{:S(2)}, u32[]{:S(2)}) %collective-permute-start.22) | collective-permute-done | bytes 393248 | tf_op jit(solution)/shard_map/ppermute | solution.py:227
  196.0 1.5 fusion.22
  198.9 9.6 %collective-permute-start.30 = (bf16[256,768]{1,0:T(8,128)(2,1)S(1)}, bf16[256,768]{1,0:T(8,128)(2,1)}, u32[]{:S(2)}, u32[]{:S(2)}) collective-permute-start(bf16[256,768]{1,0:T(8,128)(2,1)S(1)} %get-tuple-element.731), channel_id=1, source_target_pairs={{0,8},{4,12},{8,16},{12,20},{16,24},{20,28},{1,9},{5,13},{9,17},{1... | collective-permute-start | bytes 1179656 | tf_op jit(solution)/shard_map/ppermute | solution.py:227
  208.5 5.1 %collective-permute-done.31 = bf16[256,768]{1,0:T(8,128)(2,1)S(1)} collective-permute-done((bf16[256,768]{1,0:T(8,128)(2,1)S(1)}, bf16[256,768]{1,0:T(8,128)(2,1)S(1)}, u32[]{:S(2)}, u32[]{:S(2)}) %collective-permute-start.31) | collective-permute-done | bytes 393248 | tf_op jit(solution)/shard_map/ppermute | solution.py:227
  214.7 2.0 fusion.24
  218.0 5.4 %collective-permute-start.32 = (bf16[256,768]{1,0:T(8,128)(2,1)S(1)}, bf16[256,768]{1,0:T(8,128)(2,1)S(1)}, u32[]{:S(2)}, u32[]{:S(2)}) collective-permute-start(bf16[256,768]{1,0:T(8,128)(2,1)S(1)} %get-tuple-element.730), channel_id=1, source_target_pairs={{0,8},{4,12},{8,16},{12,20},{16,24},{20,28},{1,9},{5,13},{9,17},{1... | collective-permute-start | bytes 1179656 | tf_op jit(solution)/shard_map/ppermute | solution.py:227
  225.5 2.6 collective-permute-done.33
  232.6 10.4 %shard_map.142 = bf16[64,2,16,128]{3,2,1,0:T(8,128)(2,1)} custom-call(s32[64]{0:T(128)} %lengths.1, bf16[64,2,24,128]{3,2,1,0:T(8,128)(2,1)} %bitcast.240, bf16[64,192,256]{2,1,0:T(8,128)(2,1)} %keys.1, bf16[64,192,256]{2,1,0:T(8,128)(2,1)} %values.1), custom_call_target="tpu_custom_call" | custom-call | flops 201326592 | bytes 12582912 | tf_op jit(solution)/shard_map/pallas_call | solution.py:196
  245.6 6.9 %shard_map.143 = bf16[2,2560,256]{2,1,0:T(8,128)(2,1)} custom-call(bf16[5120,1024]{1,0:T(8,128)(2,1)} %all-gather.2.cloned.1.call-done.weights, bf16[1024,256]{1,0:T(8,128)(2,1)} %copy.116.heads), custom_call_target="tpu_custom_call" | custom-call | flops 2684354560 | bytes 10485760 | tf_op jit(solution)/shard_map/pallas_call | solution.py:242
  252.6 4.6 %all-to-all-start.4 = ((bf16[4,1280,256]{2,1,0:T(8,128)(2,1)}), bf16[4,1280,256]{2,1,0:T(8,128)(2,1)}, u32[]{:S(2)}, u32[]{:S(2)}) async-start(bf16[4,1280,256]{2,1,0:T(8,128)(2,1)} %bitcast.234), calls=%async_computation.4 | async-start | bytes 5242880 | tf_op jit(solution)/shard_map/all_to_all | solution.py:385
  257.2 2.5 collective-permute-start.35
  259.9 2.8 collective-permute-start.37
  262.8 3.5 %collective-permute-start.39 = (bf16[48,1280]{1,0:T(8,128)(2,1)S(1)}, bf16[48,1280]{1,0:T(8,128)(2,1)S(1)}, u32[]{:S(2)}, u32[]{:S(2)}) collective-permute-start(bf16[48,1280]{1,0:T(8,128)(2,1)S(1)} %get-tuple-element.750), channel_id=1, source_target_pairs={{0,24},{4,28},{8,16},{12,20},{16,8},{20,12},{24,0},{28,4},{1,25},{... | collective-permute-start | bytes 368648 | tf_op jit(solution)/shard_map/ppermute | solution.py:222
  267.1 3.9 %collective-permute-done.36 = bf16[48,1280]{1,0:T(8,128)(2,1)S(1)} collective-permute-done((bf16[48,1280]{1,0:T(8,128)(2,1)S(1)}, bf16[48,1280]{1,0:T(8,128)(2,1)S(1)}, u32[]{:S(2)}, u32[]{:S(2)}) %collective-permute-start.36) | collective-permute-done | bytes 122912 | tf_op jit(solution)/shard_map/ppermute | solution.py:222
  271.0 8.6 %collective-permute-done.38 = bf16[48,1280]{1,0:T(8,128)(2,1)S(1)} collective-permute-done((bf16[48,1280]{1,0:T(8,128)(2,1)S(1)}, bf16[48,1280]{1,0:T(8,128)(2,1)S(1)}, u32[]{:S(2)}, u32[]{:S(2)}) %collective-permute-start.38) | collective-permute-done | bytes 122912 | tf_op jit(solution)/shard_map/ppermute | solution.py:222
  280.3 8.4 %all-to-all-done.4 = bf16[4,1280,256]{2,1,0:T(8,128)(2,1)} async-done(((bf16[4,1280,256]{2,1,0:T(8,128)(2,1)}), bf16[4,1280,256]{2,1,0:T(8,128)(2,1)}, u32[]{:S(2)}, u32[]{:S(2)}) %all-to-all-start.4) | async-done | bytes 2621472 | tf_op jit(solution)/shard_map/all_to_all | solution.py:385
  288.7 2.2 convert_reduce_fusion.2
  291.5 1.5 collective-permute-start.43
  292.9 1.5 collective-permute-start.42
  296.5 1.5 collective-permute-done.41
  (145 shorter events, 40.5 us)
Async XLA Ops:
  11.1 7.1 %copy-start.12 = (pred[2048]{0:T(1024)(128)(4,1)}, pred[2048]{0:T(1024)(128)(4,1)S(1)}, u32[]{:S(2)}) copy-start(pred[2048]{0:T(1024)(128)(4,1)S(1)} %get-tuple-element.1168) | copy-start | bytes 6148
  12.3 11.1 %copy-start.18 = (f32[5120]{0:T(1024)S(1)}, f32[5120]{0:T(1024)}, u32[]{:S(2)}) copy-start(f32[5120]{0:T(1024)} %param.20) | copy-start | bytes 61444
  18.2 14.4 %all-to-all-start.2 = ((bf16[4,48,1280]{2,1,0:T(8,128)(2,1)}), bf16[4,48,1280]{2,1,0:T(8,128)(2,1)S(1)}, u32[]{:S(2)}, u32[]{:S(2)}) async-start(bf16[4,48,1280]{2,1,0:T(8,128)(2,1)} %bitcast.238), calls=%async_computation.2 | async-start | bytes 983040 | tf_op jit(solution)/shard_map/all_to_all | solution.py:385
  32.9 6.9 %copy-start.2 = (bf16[4,160,1024]{2,1,0:T(8,128)(2,1)S(1)}, bf16[4,160,1024]{2,1,0:T(8,128)(2,1)}, u32[]{:S(2)}) copy-start(bf16[4,160,1024]{2,1,0:T(8,128)(2,1)} %get-tuple-element.610) | copy-start | bytes 3932164
  33.9 22.1 %all-to-all-start.3 = ((bf16[8,48,640]{2,1,0:T(8,128)(2,1)}), bf16[8,48,640]{2,1,0:T(8,128)(2,1)S(1)}, u32[]{:S(2)}, u32[]{:S(2)}) async-start(bf16[8,48,640]{2,1,0:T(8,128)(2,1)} %bitcast.24), calls=%async_computation.3 | async-start | bytes 983040 | tf_op jit(solution)/shard_map/all_to_all | solution.py:385
  39.5 156.5 %all-gather.2.cloned.1.call-start = ((), (), s32[]{:S(2)}) async-start(), calls=%async_computation.5 | async-start | bytes 11796480 | tf_op jit(solution)/shard_map/all_gather | solution.py:406
  40.7 19.9 %collective-permute-start.27 = (bf16[160,1024]{1,0:T(8,128)(2,1)}, bf16[160,1024]{1,0:T(8,128)(2,1)}, u32[]{:S(2)}, u32[]{:S(2)}) collective-permute-start(bf16[160,1024]{1,0:T(8,128)(2,1)} %get-tuple-element.747), channel_id=1, source_target_pairs={{0,1},{1,0},{2,3},{3,2},{4,5},{5,4},{6,7},{7,6},{8,9},{9,8},{10,11... | collective-permute-start | bytes 983048 | tf_op jit(solution)/shard_map/ppermute | solution.py:222
  42.7 18.9 %collective-permute-start.28 = (bf16[160,1024]{1,0:T(8,128)(2,1)}, bf16[160,1024]{1,0:T(8,128)(2,1)}, u32[]{:S(2)}, u32[]{:S(2)}) collective-permute-start(bf16[160,1024]{1,0:T(8,128)(2,1)} %get-tuple-element.746), channel_id=1, source_target_pairs={{0,2},{1,3},{2,0},{3,1},{4,6},{5,7},{6,4},{7,5},{8,10},{9,11},{10,... | collective-permute-start | bytes 983048 | tf_op jit(solution)/shard_map/ppermute | solution.py:222
  44.2 18.4 %collective-permute-start.29 = (bf16[160,1024]{1,0:T(8,128)(2,1)S(1)}, bf16[160,1024]{1,0:T(8,128)(2,1)}, u32[]{:S(2)}, u32[]{:S(2)}) collective-permute-start(bf16[160,1024]{1,0:T(8,128)(2,1)S(1)} %get-tuple-element.745), channel_id=1, source_target_pairs={{0,3},{1,2},{2,1},{3,0},{4,7},{5,6},{6,5},{7,4},{8,11},{9,10},{10,... | collective-permute-start | bytes 983048 | tf_op jit(solution)/shard_map/ppermute | solution.py:222
  58.7 14.1 %collective-permute-start.11 = (bf16[160,1536]{1,0:T(8,128)(2,1)S(1)}, bf16[160,1536]{1,0:T(8,128)(2,1)S(1)}, u32[]{:S(2)}, u32[]{:S(2)}) collective-permute-start(bf16[160,1536]{1,0:T(8,128)(2,1)S(1)} %get-tuple-element.744), channel_id=1, source_target_pairs={{0,1},{1,0},{2,3},{3,2},{4,5},{5,4},{6,7},{7,6},{8,9},{9,8},{10,11... | collective-permute-start | bytes 1474568 | tf_op jit(solution)/shard_map/ppermute | solution.py:222
  64.7 35.5 %collective-permute-start.16 = (bf16[160,1536]{1,0:T(8,128)(2,1)}, bf16[160,1536]{1,0:T(8,128)(2,1)S(1)}, u32[]{:S(2)}, u32[]{:S(2)}) collective-permute-start(bf16[160,1536]{1,0:T(8,128)(2,1)} %get-tuple-element.742), channel_id=1, source_target_pairs={{0,2},{1,3},{2,0},{3,1},{4,6},{5,7},{6,4},{7,5},{8,10},{9,11},{10,... | collective-permute-start | bytes 1474568 | tf_op jit(solution)/shard_map/ppermute | solution.py:222
  66.3 34.7 %collective-permute-start.17 = (bf16[160,1536]{1,0:T(8,128)(2,1)}, bf16[160,1536]{1,0:T(8,128)(2,1)S(1)}, u32[]{:S(2)}, u32[]{:S(2)}) collective-permute-start(bf16[160,1536]{1,0:T(8,128)(2,1)} %get-tuple-element.741), channel_id=1, source_target_pairs={{0,3},{1,2},{2,1},{3,0},{4,7},{5,6},{6,5},{7,4},{8,11},{9,10},{10,... | collective-permute-start | bytes 1474568 | tf_op jit(solution)/shard_map/ppermute | solution.py:222
  72.8 31.1 %collective-permute-start.14 = (bf16[384,640]{1,0:T(8,128)(2,1)S(1)}, bf16[384,640]{1,0:T(8,128)(2,1)}, u32[]{:S(2)}, u32[]{:S(2)}) collective-permute-start(bf16[384,640]{1,0:T(8,128)(2,1)S(1)} %bitcast.246), channel_id=1, source_target_pairs={{0,3},{1,2},{2,1},{3,0},{4,7},{5,6},{6,5},{7,4},{8,11},{9,10},{10,... | collective-permute-start | bytes 1474568 | tf_op jit(solution)/shard_map/ppermute | solution.py:222
  75.7 33.3 %collective-permute-start.13 = (bf16[384,640]{1,0:T(8,128)(2,1)S(1)}, bf16[384,640]{1,0:T(8,128)(2,1)}, u32[]{:S(2)}, u32[]{:S(2)}) collective-permute-start(bf16[384,640]{1,0:T(8,128)(2,1)S(1)} %bitcast.247), channel_id=1, source_target_pairs={{0,2},{1,3},{2,0},{3,1},{4,6},{5,7},{6,4},{7,5},{8,10},{9,11},{10,... | collective-permute-start | bytes 1474568 | tf_op jit(solution)/shard_map/ppermute | solution.py:222
  86.8 22.2 %collective-permute-start.12 = (bf16[384,640]{1,0:T(8,128)(2,1)S(1)}, bf16[384,640]{1,0:T(8,128)(2,1)}, u32[]{:S(2)}, u32[]{:S(2)}) collective-permute-start(bf16[384,640]{1,0:T(8,128)(2,1)S(1)} %bitcast.248), channel_id=1, source_target_pairs={{0,1},{1,0},{2,3},{3,2},{4,5},{5,4},{6,7},{7,6},{8,9},{9,8},{10,11... | collective-permute-start | bytes 1474568 | tf_op jit(solution)/shard_map/ppermute | solution.py:222
  102.7 10.6 %collective-permute-start.18 = (bf16[640,1536]{1,0:T(8,128)(2,1)}, bf16[640,1536]{1,0:T(8,128)(2,1)}, u32[]{:S(2)}, u32[]{:S(2)}) collective-permute-start(bf16[640,1536]{1,0:T(8,128)(2,1)} %bitcast.243), channel_id=1, source_target_pairs={{0,4},{4,0},{8,12},{12,8},{16,20},{20,16},{24,28},{28,24},{1,5},{5... | collective-permute-start | bytes 5898248 | tf_op jit(solution)/shard_map/ppermute | solution.py:222
  103.9 7.9 %copy-start.19 = (f32[5120]{0:T(1024)S(1)}, f32[5120]{0:T(1024)}, u32[]{:S(2)}) copy-start(f32[5120]{0:T(1024)} %param.20) | copy-start | bytes 61444
  111.8 4.3 %collective-permute-start.15 = (bf16[1536,640]{1,0:T(8,128)(2,1)}, bf16[1536,640]{1,0:T(8,128)(2,1)}, u32[]{:S(2)}, u32[]{:S(2)}) collective-permute-start(bf16[1536,640]{1,0:T(8,128)(2,1)} %pad_maximum_fusion.2.here), channel_id=1, source_target_pairs={{0,4},{4,0},{8,12},{12,8},{16,20},{20,16},{24,28},{28,24},{1,5},{5... | collective-permute-start | bytes 5898248 | tf_op jit(solution)/shard_map/ppermute | solution.py:222
  113.3 18.1 %copy-start.13 = (pred[2048]{0:T(1024)(128)(4,1)S(1)}, pred[2048]{0:T(1024)(128)(4,1)}, u32[]{:S(2)}) copy-start(pred[2048]{0:T(1024)(128)(4,1)} %copy-done.12) | copy-start | bytes 6148
  131.4 8.6 %copy-start.17 = (s32[8,256]{1,0:T(8,128)S(1)}, s32[8,256]{1,0:T(8,128)}, u32[]{:S(2)}) copy-start(s32[8,256]{1,0:T(8,128)} %copy-done.16) | copy-start | bytes 24580
  131.4 9.1 %copy-start.9 = (s32[8,256]{1,0:T(8,128)S(1)}, s32[8,256]{1,0:T(8,128)}, u32[]{:S(2)}) copy-start(s32[8,256]{1,0:T(8,128)} %add_select_fusion.4) | copy-start | bytes 24580
  131.4 10.5 %copy-start.20 = (s32[8,256]{1,0:T(8,128)S(1)}, s32[8,256]{1,0:T(8,128)}, u32[]{:S(2)}) copy-start(s32[8,256]{1,0:T(8,128)} %add.481) | copy-start | bytes 24580
  133.5 8.8 %collective-permute-start.25 = (bf16[256,768]{1,0:T(8,128)(2,1)S(1)}, bf16[256,768]{1,0:T(8,128)(2,1)S(1)}, u32[]{:S(2)}, u32[]{:S(2)}) collective-permute-start(bf16[256,768]{1,0:T(8,128)(2,1)S(1)} %get-tuple-element.737), channel_id=1, source_target_pairs={{24,16},{28,20},{25,17},{29,21},{26,18},{30,22},{27,19},{31,23}} | collective-permute-start | bytes 1179656 | tf_op jit(solution)/shard_map/ppermute | solution.py:227
  134.2 8.1 %collective-permute-start.23 = (bf16[256,768]{1,0:T(8,128)(2,1)S(1)}, bf16[256,768]{1,0:T(8,128)(2,1)S(1)}, u32[]{:S(2)}, u32[]{:S(2)}) collective-permute-start(bf16[256,768]{1,0:T(8,128)(2,1)S(1)} %get-tuple-element.738), channel_id=1, source_target_pairs={{24,16},{28,20},{25,17},{29,21},{26,18},{30,22},{27,19},{31,23}} | collective-permute-start | bytes 1179656 | tf_op jit(solution)/shard_map/ppermute | solution.py:227
  134.8 21.6 %collective-permute-start.21 = (bf16[256,768]{1,0:T(8,128)(2,1)S(1)}, bf16[256,768]{1,0:T(8,128)(2,1)S(1)}, u32[]{:S(2)}, u32[]{:S(2)}) collective-permute-start(bf16[256,768]{1,0:T(8,128)(2,1)S(1)} %get-tuple-element.739), channel_id=1, source_target_pairs={{0,8},{4,12},{1,9},{5,13},{2,10},{6,14},{3,11},{7,15}} | collective-permute-start | bytes 1179656 | tf_op jit(solution)/shard_map/ppermute | solution.py:227
  138.6 34.4 %collective-permute-start.19 = (bf16[256,768]{1,0:T(8,128)(2,1)S(1)}, bf16[256,768]{1,0:T(8,128)(2,1)S(1)}, u32[]{:S(2)}, u32[]{:S(2)}) collective-permute-start(bf16[256,768]{1,0:T(8,128)(2,1)S(1)} %get-tuple-element.740), channel_id=1, source_target_pairs={{0,8},{4,12},{1,9},{5,13},{2,10},{6,14},{3,11},{7,15}} | collective-permute-start | bytes 1179656 | tf_op jit(solution)/shard_map/ppermute | solution.py:227
  142.2 40.8 %copy-start.4 = (bf16[192,1280]{1,0:T(8,128)(2,1)S(1)}, bf16[192,1280]{1,0:T(8,128)(2,1)}, u32[]{:S(2)}) copy-start(bf16[192,1280]{1,0:T(8,128)(2,1)} %shard_map.138) | copy-start | bytes 1474564
  175.3 13.9 %collective-permute-start.20 = (bf16[256,768]{1,0:T(8,128)(2,1)S(1)}, bf16[256,768]{1,0:T(8,128)(2,1)S(1)}, u32[]{:S(2)}, u32[]{:S(2)}) collective-permute-start(bf16[256,768]{1,0:T(8,128)(2,1)S(1)} %get-tuple-element.736), channel_id=1, source_target_pairs={{0,8},{4,12},{8,16},{12,20},{1,9},{5,13},{9,17},{13,21},{2,10},{6,... | collective-permute-start | bytes 1179656 | tf_op jit(solution)/shard_map/ppermute | solution.py:227
  179.7 16.3 %collective-permute-start.22 = (bf16[256,768]{1,0:T(8,128)(2,1)S(1)}, bf16[256,768]{1,0:T(8,128)(2,1)S(1)}, u32[]{:S(2)}, u32[]{:S(2)}) collective-permute-start(bf16[256,768]{1,0:T(8,128)(2,1)S(1)} %get-tuple-element.735), channel_id=1, source_target_pairs={{0,8},{4,12},{8,16},{12,20},{1,9},{5,13},{9,17},{13,21},{2,10},{6,... | collective-permute-start | bytes 1179656 | tf_op jit(solution)/shard_map/ppermute | solution.py:227
  181.6 14.4 %collective-permute-start.24 = (bf16[256,768]{1,0:T(8,128)(2,1)S(1)}, bf16[256,768]{1,0:T(8,128)(2,1)S(1)}, u32[]{:S(2)}, u32[]{:S(2)}) collective-permute-start(bf16[256,768]{1,0:T(8,128)(2,1)S(1)} %get-tuple-element.734), channel_id=1, source_target_pairs={{16,8},{20,12},{24,16},{28,20},{17,9},{21,13},{25,17},{29,21},{18,... | collective-permute-start | bytes 1179656 | tf_op jit(solution)/shard_map/ppermute | solution.py:227
  182.3 13.7 %collective-permute-start.26 = (bf16[256,768]{1,0:T(8,128)(2,1)S(1)}, bf16[256,768]{1,0:T(8,128)(2,1)S(1)}, u32[]{:S(2)}, u32[]{:S(2)}) collective-permute-start(bf16[256,768]{1,0:T(8,128)(2,1)S(1)} %get-tuple-element.733), channel_id=1, source_target_pairs={{16,8},{20,12},{24,16},{28,20},{17,9},{21,13},{25,17},{29,21},{18,... | collective-permute-start | bytes 1179656 | tf_op jit(solution)/shard_map/ppermute | solution.py:227
  197.6 16.0 %collective-permute-start.31 = (bf16[256,768]{1,0:T(8,128)(2,1)S(1)}, bf16[256,768]{1,0:T(8,128)(2,1)S(1)}, u32[]{:S(2)}, u32[]{:S(2)}) collective-permute-start(bf16[256,768]{1,0:T(8,128)(2,1)S(1)} %get-tuple-element.732), channel_id=1, source_target_pairs={{8,0},{12,4},{16,8},{20,12},{24,16},{28,20},{9,1},{13,5},{17,9},{2... | collective-permute-start | bytes 1179656 | tf_op jit(solution)/shard_map/ppermute | solution.py:227
  198.9 15.9 %collective-permute-start.30 = (bf16[256,768]{1,0:T(8,128)(2,1)S(1)}, bf16[256,768]{1,0:T(8,128)(2,1)}, u32[]{:S(2)}, u32[]{:S(2)}) collective-permute-start(bf16[256,768]{1,0:T(8,128)(2,1)S(1)} %get-tuple-element.731), channel_id=1, source_target_pairs={{0,8},{4,12},{8,16},{12,20},{16,24},{20,28},{1,9},{5,13},{9,17},{1... | collective-permute-start | bytes 1179656 | tf_op jit(solution)/shard_map/ppermute | solution.py:227
  216.7 11.3 %collective-permute-start.33 = (bf16[256,768]{1,0:T(8,128)(2,1)S(1)}, bf16[256,768]{1,0:T(8,128)(2,1)S(1)}, u32[]{:S(2)}, u32[]{:S(2)}) collective-permute-start(bf16[256,768]{1,0:T(8,128)(2,1)S(1)} %get-tuple-element.729), channel_id=1, source_target_pairs={{8,0},{12,4},{16,8},{20,12},{24,16},{28,20},{9,1},{13,5},{17,9},{2... | collective-permute-start | bytes 1179656 | tf_op jit(solution)/shard_map/ppermute | solution.py:227
  218.0 11.2 %collective-permute-start.32 = (bf16[256,768]{1,0:T(8,128)(2,1)S(1)}, bf16[256,768]{1,0:T(8,128)(2,1)S(1)}, u32[]{:S(2)}, u32[]{:S(2)}) collective-permute-start(bf16[256,768]{1,0:T(8,128)(2,1)S(1)} %get-tuple-element.730), channel_id=1, source_target_pairs={{0,8},{4,12},{8,16},{12,20},{16,24},{20,28},{1,9},{5,13},{9,17},{1... | collective-permute-start | bytes 1179656 | tf_op jit(solution)/shard_map/ppermute | solution.py:227
  252.6 10.2 %collective-permute-start.34 = (bf16[48,1280]{1,0:T(8,128)(2,1)S(1)}, bf16[48,1280]{1,0:T(8,128)(2,1)S(1)}, u32[]{:S(2)}, u32[]{:S(2)}) collective-permute-start(bf16[48,1280]{1,0:T(8,128)(2,1)S(1)} %get-tuple-element.755), channel_id=1, source_target_pairs={{0,4},{4,0},{8,12},{12,8},{16,20},{20,16},{24,28},{28,24},{1,5},{5... | collective-permute-start | bytes 368648 | tf_op jit(solution)/shard_map/ppermute | solution.py:222
  252.6 36.1 %all-to-all-start.4 = ((bf16[4,1280,256]{2,1,0:T(8,128)(2,1)}), bf16[4,1280,256]{2,1,0:T(8,128)(2,1)}, u32[]{:S(2)}, u32[]{:S(2)}) async-start(bf16[4,1280,256]{2,1,0:T(8,128)(2,1)} %bitcast.234), calls=%async_computation.4 | async-start | bytes 5242880 | tf_op jit(solution)/shard_map/all_to_all | solution.py:385
  257.2 9.1 %collective-permute-start.35 = (bf16[48,1280]{1,0:T(8,128)(2,1)S(1)}, bf16[48,1280]{1,0:T(8,128)(2,1)S(1)}, u32[]{:S(2)}, u32[]{:S(2)}) collective-permute-start(bf16[48,1280]{1,0:T(8,128)(2,1)S(1)} %get-tuple-element.754), channel_id=1, source_target_pairs={{0,8},{4,12},{8,0},{12,4},{16,24},{20,28},{24,16},{28,20},{1,9},{5... | collective-permute-start | bytes 368648 | tf_op jit(solution)/shard_map/ppermute | solution.py:222
  259.8 11.2 %collective-permute-start.36 = (bf16[48,1280]{1,0:T(8,128)(2,1)S(1)}, bf16[48,1280]{1,0:T(8,128)(2,1)S(1)}, u32[]{:S(2)}, u32[]{:S(2)}) collective-permute-start(bf16[48,1280]{1,0:T(8,128)(2,1)S(1)} %get-tuple-element.753), channel_id=1, source_target_pairs={{0,12},{4,8},{8,4},{12,0},{16,28},{20,24},{24,20},{28,16},{1,13},{... | collective-permute-start | bytes 368648 | tf_op jit(solution)/shard_map/ppermute | solution.py:222
  259.9 11.0 %collective-permute-start.37 = (bf16[48,1280]{1,0:T(8,128)(2,1)S(1)}, bf16[48,1280]{1,0:T(8,128)(2,1)S(1)}, u32[]{:S(2)}, u32[]{:S(2)}) collective-permute-start(bf16[48,1280]{1,0:T(8,128)(2,1)S(1)} %get-tuple-element.752), channel_id=1, source_target_pairs={{0,16},{4,20},{8,24},{12,28},{16,0},{20,4},{24,8},{28,12},{1,17},{... | collective-permute-start | bytes 368648 | tf_op jit(solution)/shard_map/ppermute | solution.py:222
  262.8 16.8 %collective-permute-start.38 = (bf16[48,1280]{1,0:T(8,128)(2,1)S(1)}, bf16[48,1280]{1,0:T(8,128)(2,1)S(1)}, u32[]{:S(2)}, u32[]{:S(2)}) collective-permute-start(bf16[48,1280]{1,0:T(8,128)(2,1)S(1)} %get-tuple-element.751), channel_id=1, source_target_pairs={{0,20},{4,16},{8,28},{12,24},{16,4},{20,0},{24,12},{28,8},{1,21},{... | collective-permute-start | bytes 368648 | tf_op jit(solution)/shard_map/ppermute | solution.py:222
  262.8 16.8 %collective-permute-start.39 = (bf16[48,1280]{1,0:T(8,128)(2,1)S(1)}, bf16[48,1280]{1,0:T(8,128)(2,1)S(1)}, u32[]{:S(2)}, u32[]{:S(2)}) collective-permute-start(bf16[48,1280]{1,0:T(8,128)(2,1)S(1)} %get-tuple-element.750), channel_id=1, source_target_pairs={{0,24},{4,28},{8,16},{12,20},{16,8},{20,12},{24,0},{28,4},{1,25},{... | collective-permute-start | bytes 368648 | tf_op jit(solution)/shard_map/ppermute | solution.py:222
  266.4 13.3 %collective-permute-start.40 = (bf16[48,1280]{1,0:T(8,128)(2,1)S(1)}, bf16[48,1280]{1,0:T(8,128)(2,1)S(1)}, u32[]{:S(2)}, u32[]{:S(2)}) collective-permute-start(bf16[48,1280]{1,0:T(8,128)(2,1)S(1)} %get-tuple-element.749), channel_id=1, source_target_pairs={{0,28},{4,24},{8,20},{12,16},{16,12},{20,8},{24,4},{28,0},{1,29},{... | collective-permute-start | bytes 368648 | tf_op jit(solution)/shard_map/ppermute | solution.py:222
  280.3 10.7 %copy-start.11 = (s32[2048]{0:T(1024)S(1)}, s32[2048]{0:T(1024)}, u32[]{:S(2)}) copy-start(s32[2048]{0:T(1024)} %copy-done.10) | copy-start | bytes 24580
  280.3 10.7 %copy-start.15 = (pred[2048]{0:T(1024)(128)(4,1)S(1)}, pred[2048]{0:T(1024)(128)(4,1)}, u32[]{:S(2)}) copy-start(pred[2048]{0:T(1024)(128)(4,1)} %copy-done.12) | copy-start | bytes 6148
  291.5 4.5 %collective-permute-start.43 = (f32[256]{0:T(256)S(1)}, f32[256]{0:T(256)S(1)}, u32[]{:S(2)}, u32[]{:S(2)}) collective-permute-start(f32[256]{0:T(256)S(1)} %multiply_reduce_fusion), channel_id=1, source_target_pairs={{0,3},{1,2},{2,1},{3,0},{4,7},{5,6},{6,5},{7,4},{8,11},{9,10},{10,... | collective-permute-start | bytes 3080 | tf_op jit(solution)/shard_map/ppermute | solution.py:222
  292.9 3.6 %collective-permute-start.42 = (f32[256]{0:T(256)S(1)}, f32[256]{0:T(256)S(1)}, u32[]{:S(2)}, u32[]{:S(2)}) collective-permute-start(f32[256]{0:T(256)S(1)} %multiply_reduce_fusion), channel_id=1, source_target_pairs={{0,2},{1,3},{2,0},{3,1},{4,6},{5,7},{6,4},{7,5},{8,10},{9,11},{10,... | collective-permute-start | bytes 3080 | tf_op jit(solution)/shard_map/ppermute | solution.py:222
  294.4 3.6 %collective-permute-start.41 = (f32[256]{0:T(256)S(1)}, f32[256]{0:T(256)S(1)}, u32[]{:S(2)}, u32[]{:S(2)}) collective-permute-start(f32[256]{0:T(256)S(1)} %multiply_reduce_fusion), channel_id=1, source_target_pairs={{0,1},{1,0},{2,3},{3,2},{4,5},{5,4},{6,7},{7,6},{8,9},{9,8},{10,11... | collective-permute-start | bytes 3080 | tf_op jit(solution)/shard_map/ppermute | solution.py:222
  (4 other events, 7.1 us)
Sparse Core Ops, SparseCore 0:
  64.9 111.0 all-gather.1
